TPU v7x, 32 devices: a whole 2x2x4 slice. The times are simulated.
32 devices in a mesh: view: 2 (over y), slab: 16 (over z, x, core).
Axes of the slice: x: 2, y: 2, z: 4, core: 2. Of those that a mesh axis runs over, the one named last changes fastest.
Arguments:
- estimate: float32 [16, 256, 1024], P('slab'), may hold values from 0.5 to 2
- measured: float32 [2, 16, 256, 1024], P('view', None, 'slab'), may hold values from 0.5 to 2
- offsets: int32 [2], P('view'), may hold values from 0 to 15, as said below
- mirrors: int32 [2, 2], P('view'), may hold values from 0 to 1
- psf: float32 [2, 3, 17], P('view'), may hold values from 0.002 to 1, as said below
Outputs:
- updated: float32 [16, 256, 1024], P('slab')
Inputs may be any that keep to these rules, and one draw needn't show every extreme that they name: `psf`: every tap is positive. The views' offsets are distinct, and one view has the last block offset.
All inputs are finite; a program needn't handle non-finite values.
Results may differ from a plain program's by a relative error of at most 0.0003.
Values sent between devices are 32-bit elements; how exact they have to be, the bound alone decides.
No kernel may reach another device: no remote copies, remote signals or barrier semaphores. Data moves between devices by JAX's collectives and lax.ppermute only.
A program may use at most 64 MiB of HBM per device.

v0:
```python
import jax
import jax.numpy as jnp
from jax import lax
from jax.sharding import PartitionSpec as P

BLOCK = 64


def with_halo(cells, sides, width):
    for axis, dim in sides:
        count = lax.axis_size(axis)
        ends = count - 1
        head = lax.slice_in_dim(cells, 0, width, axis=dim)
        tail = lax.slice_in_dim(cells, cells.shape[dim] - width, cells.shape[dim], axis=dim)
        cells = jnp.concatenate(
            [
                lax.ppermute(tail, axis, [(i, (i + 1) % count) for i in range(ends)]),
                cells,
                lax.ppermute(head, axis, [((i + 1) % count, i) for i in range(ends)]),
            ],
            axis=dim,
        )
    return cells


def convolve(volume, tap_row, axis_dim, reverse, padding):
    tap_count = tap_row.shape[0]
    radius = tap_count // 2
    if reverse:
        tap_row = tap_row[::-1]
    if padding:
        widths = [(0, 0)] * volume.ndim
        widths[axis_dim] = (radius, radius)
        volume = jnp.pad(volume, widths)
    length = volume.shape[axis_dim] - 2 * radius
    summed = tap_row[0] * lax.slice_in_dim(volume, 0, length, axis=axis_dim)
    for tap_index in range(1, tap_count):
        summed = summed + tap_row[tap_index] * lax.slice_in_dim(
            volume, tap_index, tap_index + length, axis=axis_dim
        )
    return summed


def resample(volume, shift_blocks, mirror_z, mirror_x):
    volume = lax.cond(mirror_z == 1, lambda arr: jnp.flip(arr, 0), lambda arr: arr, volume)
    volume = lax.cond(mirror_x == 1, lambda arr: jnp.flip(arr, 2), lambda arr: arr, volume)
    return jnp.roll(volume, shift_blocks * BLOCK, axis=2)


def unresample(volume, shift_blocks, mirror_z, mirror_x):
    volume = jnp.roll(volume, -shift_blocks * BLOCK, axis=2)
    volume = lax.cond(mirror_x == 1, lambda arr: jnp.flip(arr, 2), lambda arr: arr, volume)
    return lax.cond(mirror_z == 1, lambda arr: jnp.flip(arr, 0), lambda arr: arr, volume)


def body(estimate, measured, offsets, mirrors, psf):
    radius = psf.shape[2] // 2
    moved = lax.all_to_all(estimate, "slab", split_axis=1, concat_axis=0, tiled=True)
    rimmed = with_halo(moved, (("slab", 1),), radius)
    filtered = convolve(rimmed, psf[0, 1], 1, False, False)
    framed = resample(filtered, offsets[0], mirrors[0, 0], mirrors[0, 1])
    blurred = convolve(framed, psf[0, 0], 0, False, True)
    blurred = convolve(blurred, psf[0, 2], 2, False, True)
    ratio = measured[0] / blurred
    spread = convolve(ratio, psf[0, 2], 2, True, True)
    spread = convolve(spread, psf[0, 0], 0, True, True)
    corrections = [unresample(spread, offsets[0], mirrors[0, 0], mirrors[0, 1])]
    returned = lax.all_to_all(
        jnp.stack(corrections), "slab", split_axis=1, concat_axis=2, tiled=True
    )
    local_product = convolve(returned[0], psf[0, 1], 1, True, True)
    gathered = lax.all_gather(local_product[None], "view", axis=0, tiled=True)
    factor = jnp.prod(gathered, axis=0)
    return estimate * factor


def solution(mesh):
    placed = (
        P("slab", None, None),
        P("view", None, "slab", None),
        P("view"),
        P("view", None),
        P("view", None, None),
    )
    return jax.shard_map(
        body, mesh=mesh, in_specs=placed, out_specs=P("slab", None, None), check_vma=False
    )
```

profile of v0, /device:TPU:0, one launch (start us, length us, event | category | flops | bytes accessed | tf_op | source)
XLA Modules:
  0.0 213.9 jit_solution(11371689109838763911)
XLA Ops:
  6.5 0.0 all-gather.3.cloned.1.call-start
  6.5 2.3 %copy.7 = f32[1,256,1024]{2,0,1:T(1,128)S(1)} copy(f32[1,256,1024]{2,1,0:T(8,128)} %param.15) | data formatting | bytes 2097152 | tf_op args[0]
  8.8 32.0 %all_to_all.21 = f32[1,256,1024]{2,0,1:T(1,128)S(1)} all-to-all(f32[1,256,1024]{2,0,1:T(1,128)S(1)} %copy.7), channel_id=1, replica_groups=mesh['view'=2,'slab'=16] {'slab'}, dimensions={1} | all-to-all | bytes 2097152 | tf_op jit(solution)/shard_map/all_to_all | solution.py:58
  40.8 0.0 copy-start.3
  40.9 0.0 copy-start.2
  40.9 0.2 copy.8
  41.1 0.1 fusion.190
  41.2 2.7 %collective-permute-start = (f32[16,8,1024]{2,1,0:T(8,128)S(1)}, f32[16,8,1024]{2,1,0:T(8,128)S(1)}, u32[]{:S(2)}, u32[]{:S(2)}) collective-permute-start(f32[16,8,1024]{2,1,0:T(8,128)S(1)} %get-tuple-element.26), channel_id=1, source_target_pairs={{0,1},{1,2},{2,3},{3,4},{4,5},{5,6},{6,7},{7,8},{8,9},{9,10},{10,1... | collective-permute-start | bytes 1572872 | tf_op jit(solution)/shard_map/ppermute | solution.py:17
  43.9 1.3 collective-permute-start.1
  45.9 0.0 copy-done.3
  45.9 0.6 fusion.194
  47.7 0.0 copy-done.2
  47.8 0.7 fusion.193
  48.5 0.7 fusion.192
  49.2 0.7 fusion.191
  49.9 0.0 collective-permute-done
  49.9 0.0 collective-permute-done.1
  49.9 13.7 %fusion.70 = f32[16,16,1024]{2,1,0:T(8,128)S(1)} fusion(f32[16,16,1024]{2,1,0:T(8,128)S(1)} %bitcast.64, f32[16,8,1024]{2,1,0:T(8,128)S(1)} %collective-permute-done.1, f32[16,8,1024]{2,1,0:T(8,128)S(1)} %collective-permute-done, f32[]{:T(128)} %bitcast, f32[]{:T(128)} %bitcast.23, f32[]{:T(128)} %bitcast.22, f32[]{:T(128)} %bitcast.21, f32[]{:T(128)} %bitcast.20, ...), kind=kLoop, calls=%fused_computation.166 | loop fusion | flops 12845056 | bytes 3145796 | tf_op jit(solution)/shard_map/add | solution.py:38
  63.6 0.2 conditional.5
  63.8 0.0 copy-start.1
  63.8 0.6 fusion.66
  64.4 12.1 %fusion.127 = f32[16,16,1024]{2,1,0:T(8,128)S(1)} fusion(f32[16,16,1024]{2,1,0:T(8,128)S(1)} %fusion.66, f32[]{:T(128)} %bitcast.39, f32[]{:T(128)} %bitcast.38, f32[]{:T(128)} %bitcast.37, f32[]{:T(128)} %bitcast.36, f32[]{:T(128)} %bitcast.35, f32[]{:T(128)} %bitcast.34, f32[]{:T(128)} %bitcast.33, f32[]{:T(128)} %bitcast.32, f32[]{:T(128)} %bitcast.31, ...), kind=kLoop, calls=%fused_computation.223 | loop fusion | flops 8650752 | bytes 2097220 | tf_op jit(solution)/shard_map/add | solution.py:38
  76.6 0.0 copy-done.1
  76.6 15.1 %fusion.17 = f32[16,16,1024]{2,1,0:T(8,128)S(1)} fusion(f32[16,16,1024]{2,1,0:T(8,128)S(1)} %fusion.127, f32[1,16,16,1024]{3,2,1,0:T(8,128)S(1)} %copy-done.1, f32[]{:T(128)} %bitcast.54, f32[]{:T(128)} %bitcast.53, f32[]{:T(128)} %bitcast.52, f32[]{:T(128)} %bitcast.51, f32[]{:T(128)} %bitcast.50, f32[]{:T(128)} %bitcast.49, f32[]{:T(128)} %bitcast.48, ...), kind=kLoop, calls=%fused_computation.113 | loop fusion | flops 8912896 | bytes 3145796 | tf_op jit(solution)/shard_map/div | solution.py:64
  91.7 15.1 %fusion.49 = f32[16,16,1024]{2,1,0:T(8,128)S(1)} fusion(f32[16,16,1024]{2,1,0:T(8,128)S(1)} %fusion.17, f32[]{:T(128)} %bitcast.54, f32[]{:T(128)} %bitcast.53, f32[]{:T(128)} %bitcast.52, f32[]{:T(128)} %bitcast.51, f32[]{:T(128)} %bitcast.50, f32[]{:T(128)} %bitcast.49, f32[]{:T(128)} %bitcast.48, f32[]{:T(128)} %bitcast.47, f32[]{:T(128)} %bitcast.46, ...), kind=kLoop, calls=%fused_computation.145 | loop fusion | flops 8650752 | bytes 2097220 | tf_op jit(solution)/shard_map/add | solution.py:38
  106.8 12.1 %fusion.159 = f32[16,16,1024]{2,1,0:T(8,128)S(1)} fusion(f32[16,16,1024]{2,1,0:T(8,128)S(1)} %fusion.49, f32[]{:T(128)} %bitcast.39, f32[]{:T(128)} %bitcast.38, f32[]{:T(128)} %bitcast.37, f32[]{:T(128)} %bitcast.36, f32[]{:T(128)} %bitcast.35, f32[]{:T(128)} %bitcast.34, f32[]{:T(128)} %bitcast.33, f32[]{:T(128)} %bitcast.32, f32[]{:T(128)} %bitcast.31, ...), kind=kLoop, calls=%fused_computation.255 | loop fusion | flops 8650752 | bytes 2097220 | tf_op jit(solution)/shard_map/add | solution.py:38
  118.9 0.6 fusion.65
  119.6 36.8 %all_to_all.22 = f32[1,16,16,1024]{3,2,0,1:T(8,128)S(1)} all-to-all(f32[1,16,16,1024]{3,2,0,1:T(8,128)S(1)} %bitcast.62), channel_id=1, replica_groups=mesh['view'=2,'slab'=16] {'slab'}, dimensions={1} | all-to-all | bytes 2097152 | tf_op jit(solution)/shard_map/all_to_all | solution.py:68
  156.4 13.6 %multiply_add_fusion = f32[1,256,1024]{2,1,0:T(8,128)} fusion(f32[1,256,1024]{2,1,0:T(8,128)S(1)} %bitcast.65, f32[]{:T(128)} %bitcast.8, f32[]{:T(128)} %bitcast.9, f32[]{:T(128)} %bitcast.10, f32[]{:T(128)} %bitcast.11, f32[]{:T(128)} %bitcast.12, f32[]{:T(128)} %bitcast.13, f32[]{:T(128)} %bitcast.14, f32[]{:T(128)} %bitcast.15, f32[]{:T(128)} %bitcast.16, ...), kind=kLoop, calls=%fused_computation.276 | loop fusion | flops 8650752 | bytes 2097220 | tf_op jit(solution)/shard_map/add | solution.py:38
  170.0 0.0 copy-start
  170.0 0.0 all-gather.3.cloned.1.call-update
  170.0 34.1 %all-gather.3.cloned.1.call-done = f32[2,256,1024]{2,1,0:T(8,128)} async-done(((f32[1,256,1024]{2,1,0:T(8,128)}), f32[2,256,1024]{2,1,0:T(8,128)}) %all-gather.3.cloned.1.call-update) | async-done | bytes 2097168 | tf_op jit(solution)/shard_map/all_gather | solution.py:72
  204.1 1.8 reduce.1
  205.9 0.0 copy-done
  205.9 1.1 bitcast_multiply_fusion
  (3 shorter events, 0.0 us)
Async XLA Ops:
  6.5 197.5 %all-gather.3.cloned.1.call-start = ((), (), s32[]{:S(2)}) async-start(), calls=%async_computation.2 | async-start | bytes 3145728 | tf_op jit(solution)/shard_map/all_gather | solution.py:72
  40.8 5.0 %copy-start.3 = (s32[1,2]{1,0:T(1,128)S(1)}, s32[1,2]{1,0:T(1,128)}, u32[]{:S(2)}) copy-start(s32[1,2]{1,0:T(1,128)} %param.18) | copy-start | bytes 28
  40.9 6.9 %copy-start.2 = (f32[1,3,17]{2,0,1:T(1,128)S(1)}, f32[1,3,17]{2,0,1:T(1,128)}, u32[]{:S(2)}) copy-start(f32[1,3,17]{2,0,1:T(1,128)} %param.19) | copy-start | bytes 616
  41.2 8.8 %collective-permute-start = (f32[16,8,1024]{2,1,0:T(8,128)S(1)}, f32[16,8,1024]{2,1,0:T(8,128)S(1)}, u32[]{:S(2)}, u32[]{:S(2)}) collective-permute-start(f32[16,8,1024]{2,1,0:T(8,128)S(1)} %get-tuple-element.26), channel_id=1, source_target_pairs={{0,1},{1,2},{2,3},{3,4},{4,5},{5,6},{6,7},{7,8},{8,9},{9,10},{10,1... | collective-permute-start | bytes 1572872 | tf_op jit(solution)/shard_map/ppermute | solution.py:17
  43.9 6.0 %collective-permute-start.1 = (f32[16,8,1024]{2,1,0:T(8,128)S(1)}, f32[16,8,1024]{2,1,0:T(8,128)S(1)}, u32[]{:S(2)}, u32[]{:S(2)}) collective-permute-start(f32[16,8,1024]{2,1,0:T(8,128)S(1)} %get-tuple-element.27), channel_id=1, source_target_pairs={{1,0},{2,1},{3,2},{4,3},{5,4},{6,5},{7,6},{8,7},{9,8},{10,9},{11,1... | collective-permute-start | bytes 1572872 | tf_op jit(solution)/shard_map/ppermute | solution.py:19
  63.8 12.8 %copy-start.1 = (f32[1,16,16,1024]{3,2,1,0:T(8,128)S(1)}, f32[1,16,16,1024]{3,2,1,0:T(8,128)}, u32[]{:S(2)}) copy-start(f32[1,16,16,1024]{3,2,1,0:T(8,128)} %param.16) | copy-start | bytes 3145732
  170.0 35.9 %copy-start = (f32[1,256,1024]{2,1,0:T(8,128)S(1)}, f32[1,256,1024]{2,1,0:T(8,128)}, u32[]{:S(2)}) copy-start(f32[1,256,1024]{2,1,0:T(8,128)} %param.15) | copy-start | bytes 3145732
Sparse Core Ops, SparseCore 0:
  170.1 33.8 all-gather.2
where the time goes:
time: 215 us; the launch traced here: 214 us
  other arithmetic  85.9 us (40%)
  blocking collectives  68.8 us (32%)
  waiting for transfers between devices  34.1 us (16%)
  between operations  15.5 us (7%)
  local copies, waits for them, and re-layouts  5.36 us (2%)
  starting transfers between devices  4 us (2%)
    add x5, other arithmetic, convolve(): summed + tap_row[tap_index] * lax.slice_in_dim(volume, tap_index, tap_ind...  66.6 us
    all_to_all x1, blocking collectives, body(): lax.all_to_all(jnp.stack(corrections), 'slab', split_axis=1, concat_axis=...  36.8 us
    all_gather x1, waiting for transfers between devices, body(): gathered = lax.all_gather(local_product[None], 'view', axis=0, tiled=True)  34.1 us
    all_to_all x1, blocking collectives, body(): lax.all_to_all(estimate, 'slab', split_axis=1, concat_axis=0, tiled=True)  32 us
    div x1, other arithmetic, body(): ratio = measured[0] / blurred  15.1 us
  transfers between devices with their start and end apart: 3, of which 1 were waited for; matrix products, arithmetic and copies ran while one was open for 1% of the time, Pallas kernels for 0%

commit v1 on v0

v1 whole, which is shorter than its diff:
```python
import functools

import jax
import jax.numpy as jnp
from jax import lax
from jax.experimental import pallas as pl
from jax.experimental.pallas import tpu as pltpu
from jax.sharding import PartitionSpec as P

BLOCK = 64
TILE = 256
LANES = 128
CHUNKS = 2
LOW = 4
PACKED = 16
RATIO_BYTES = 12 * 1024 * 1024
OTHER_BYTES = 6 * 1024 * 1024
VMEM_BYTES = 48 * 1024 * 1024


def split(value):
    high = value.astype(jnp.bfloat16)
    low = (value - high.astype(jnp.float32)).astype(jnp.bfloat16)
    return high, low


def dot3(left, right):
    def dot(a, b):
        return jnp.dot(a, b, preferred_element_type=jnp.float32)

    return dot(left[0], right[0]) + (dot(left[0], right[1]) + dot(left[1], right[0]))


def toeplitz(taps, place):
    out = jnp.zeros(place.shape, jnp.float32)
    for index, tap in enumerate(taps):
        out = jnp.where(place == index, tap, out)
    return out


def y_cells(index, start, rows, chunks):
    step = rows // chunks
    count = index.shape[0] * index.shape[1] // chunks
    chunk = index // count
    within = index % count
    return start + (within // step) * rows + chunk * step + within % step


def y_band(taps, targets, sources):
    return split(toeplitz(taps, sources - targets + len(taps) // 2))


def y_window(first, height):
    window = min(2 * TILE, height)
    if height <= TILE:
        return 0, window
    return pl.multiple_of(jnp.clip(first - LANES, 0, height - window), LANES), window


def taps_of(psf_ref, row):
    return [psf_ref[0, row, t] for t in range(psf_ref.shape[2])]


def iota(shape, dimension):
    return lax.broadcasted_iota(jnp.int32, shape, dimension)


THERE = ("lh", "hl")
BACK = ("lh", "hl")


def order_of(plan, chunk, slabs):
    digits = {"l": (LOW, 1), "h": (slabs // LOW, LOW)}
    return tuple(digits[name] for name in plan[chunk])


def place_of(index, plan, chunk, slabs):
    return tuple(index // unit % radix for radix, unit in order_of(plan, chunk, slabs))


def first_message(plan, chunk, slabs, stage):
    return sum(order_of(plan, c, slabs)[stage][0] for c in range(chunk))


def blur_y_kernel(chunk, psf_ref, est_ref, *refs):
    out_refs = refs[-LOW:] if THERE[chunk] == "lh" else refs
    me = lax.axis_index("slab")
    height, width = est_ref.shape[1:]
    step = out_refs[0].shape[1]
    rows = step * CHUNKS
    slabs = height // rows
    lines = min(TILE, height) // CHUNKS
    blocks = lines // step
    taps = taps_of(psf_ref, 1)
    line = iota((lines, 1), 0)
    for group in range(slabs // blocks):
        targets = ((line // step + group * blocks) ^ me) * rows + chunk * step + line % step
        first = ((group * blocks) ^ (me // blocks * blocks)) * rows
        start, window = y_window(first, height)
        band = y_band(taps, targets, start + iota((1, window), 1))
        for x in range(0, width, TILE):
            value = dot3(band, split(est_ref[0, pl.ds(start, window), x : x + TILE]))
            for block in range(blocks):
                message, at = place_of(group * blocks + block, THERE, chunk, slabs)
                out_refs[message][at, :, x : x + TILE] = value[block * step : (block + 1) * step]


def x_position(cell, width, shift, flip):
    place = jnp.where(flip, width - 1 - cell, cell) + shift
    return jnp.where(place >= width, place - width, place)


def ratio_kernel(chunk, offset_ref, mirror_ref, psf_ref, meas_ref, *refs):
    work_ref, out_ref, high_ref, low_ref = refs[-4:]
    me = lax.axis_index("slab")
    depth, rows, width = work_ref.shape
    last = order_of(THERE, chunk, depth)[-1][0]
    arrived, leaving = refs[:last], refs[last:-4]
    for index in range(depth):
        at, message = place_of(index, THERE, chunk, depth)
        work_ref[me ^ index] = arrived[message][at]
    tap_count = psf_ref.shape[2]
    radius = tap_count // 2
    flip_z = mirror_ref[0, 0] == 1
    flip_x = mirror_ref[0, 1] == 1
    shift = offset_ref[0] * BLOCK

    def oriented(row, flip):
        taps = taps_of(psf_ref, row)
        return [jnp.where(flip, taps[tap_count - 1 - t], taps[t]) for t in range(tap_count)]

    z_taps = oriented(0, flip_z)
    x_taps = oriented(2, flip_x)

    def filter_z(load, store, taps):
        for z in range(depth):
            total = None
            for t in range(tap_count):
                source = z + t - radius
                if 0 <= source < depth:
                    term = taps[t] * load(source)
                    total = term if total is None else total + term
            store(z, total)

    group = max(1, PACKED // rows)

    @pl.loop(0, width // LANES)
    def _(index):
        lanes = pl.ds(pl.multiple_of(index * LANES, LANES), LANES)
        inner = pl.ds(pl.multiple_of((index + 1) * LANES, LANES), LANES)
        held = []

        def put(z, value):
            held.append(value)
            if len(held) == group:
                high, low = split(jnp.concatenate(held))
                where = pl.ds((z + 1 - group) * rows, group * rows)
                high_ref[where, inner] = high
                low_ref[where, inner] = low
                held.clear()

        filter_z(lambda z: work_ref[z, :, lanes], put, z_taps)

    def wrap():
        for ref in (high_ref, low_ref):
            ref[:, 0:LANES] = ref[:, width : width + LANES]
            ref[:, width + LANES : width + 2 * LANES] = ref[:, LANES : 2 * LANES]

    window = TILE + 2 * LANES
    shape = (window, TILE)
    place = (
        lax.broadcasted_iota(jnp.int32, shape, 0)
        - lax.broadcasted_iota(jnp.int32, shape, 1)
        + (radius - LANES)
    )
    bands = (toeplitz(x_taps, place), toeplitz(x_taps[::-1], place))
    lines = depth * rows
    lines_at = min(TILE, lines)
    top = chunk * rows

    def filter_x(band, store):
        wrap()
        for x in range(0, width, TILE):
            source = (lax.broadcasted_iota(jnp.int32, (window, 1), 0) + (x - LANES + width)) % width
            target = lax.broadcasted_iota(jnp.int32, (1, TILE), 1) + x
            apart = x_position(source, width, shift, flip_x) - x_position(target, width, shift, flip_x)
            cut = split(jnp.where(jnp.abs(apart) <= radius, band, 0.0))
            for line in range(0, lines, lines_at):
                at = slice(line, line + lines_at)
                cells = (high_ref[at, x : x + window], low_ref[at, x : x + window])
                store(line, x, dot3(cells, cut))

    blurred = {}

    def keep(line, x, value):
        blurred[line, x] = value

    filter_x(bands[0], keep)
    for (line, x), value in blurred.items():
        seen = meas_ref[line // rows : (line + lines_at) // rows, top : top + rows, x : x + TILE]
        high, low = split(seen.reshape(lines_at, TILE) / value)
        high_ref[line : line + lines_at, x + LANES : x + LANES + TILE] = high
        low_ref[line : line + lines_at, x + LANES : x + LANES + TILE] = low

    def keep_spread(line, x, value):
        work_ref[line // rows : (line + lines_at) // rows, :, x : x + TILE] = value.reshape(
            lines_at // rows, rows, TILE
        )

    filter_x(bands[1], keep_spread)

    @pl.loop(0, width // LANES)
    def _(index):
        lanes = pl.ds(pl.multiple_of(index * LANES, LANES), LANES)

        def store(z, value):
            out_ref[z, :, lanes] = value

        filter_z(lambda z: work_ref[z, :, lanes], store, z_taps[::-1])

    for index in range(depth):
        message, at = place_of(index, BACK, chunk, depth)
        leaving[message][at] = out_ref[me ^ index]


def product_kernel(psf_ref, factor_ref, *refs):
    me = lax.axis_index("slab")
    out_ref, work_ref = refs[-2:]
    chunks, slabs, step, width = work_ref.shape
    rows = step * chunks
    height = slabs * rows
    for chunk in range(chunks):
        for index in range(slabs):
            at, message = place_of(index, BACK, chunk, slabs)
            work_ref[chunk, me ^ index] = refs[first_message(BACK, chunk, slabs, -1) + message][at]
    taps = taps_of(psf_ref, 1)[::-1]
    lines = min(TILE, height)

    def block(first):
        start, window = y_window(first, height)
        targets = first + iota((lines, 1), 0)
        sources = y_cells(iota((1, window), 1), start, rows, chunks)
        band = y_band(taps, targets, sources)
        place, where = pl.ds(first, lines), pl.ds(start // rows, window // rows)
        for x in range(0, width, TILE):
            at = slice(x, x + TILE)
            cells = jnp.concatenate(
                [
                    work_ref[chunk, where, :, at].reshape(window // chunks, TILE)
                    for chunk in range(chunks)
                ]
            )
            out_ref[0, place, at] = factor_ref[0, place, at] * dot3(band, split(cells))

    if height == lines:
        block(0)
    else:
        pl.loop(0, height // lines)(lambda index: block(pl.multiple_of(index * lines, lines)))


SCALARS = pl.BlockSpec(memory_space=pltpu.SMEM)
WHOLE = pl.BlockSpec(memory_space=pltpu.VMEM)
PARAMS = pltpu.CompilerParams(vmem_limit_bytes=VMEM_BYTES)


def cost(moved):
    return pl.CostEstimate(flops=0, bytes_accessed=moved, transcendentals=0)


def body(estimate, measured, offsets, mirrors, psf):
    views = lax.axis_size("view")
    slabs = lax.axis_size("slab")
    _, height, width = estimate.shape
    _, depth, rows, _ = measured.shape
    step = rows // CHUNKS
    swap = [(i, (i + 1) % views) for i in range(views)]

    def shapes(plan, chunk):
        (first, _), (second, _) = order_of(plan, chunk, slabs)
        return [jax.ShapeDtypeStruct((second, step, width), jnp.float32)] * first

    def send(parts, unit):
        return [
            lax.ppermute(part, "slab", [(i, i ^ (k * unit)) for i in range(slabs)]) if k else part
            for k, part in enumerate(parts)
        ]

    def exchange(parts, plan, chunk):
        (_, first_unit), (second, second_unit) = order_of(plan, chunk, slabs)
        parts = send(parts, first_unit)
        return send([jnp.stack([part[at] for part in parts]) for at in range(second)], second_unit)

    sent = [None] * CHUNKS
    for chunk in reversed(range(CHUNKS)):
        order = [] if chunk == CHUNKS - 1 else sent[chunk + 1][:1]
        sent[chunk] = pl.pallas_call(
            functools.partial(blur_y_kernel, chunk),
            out_shape=shapes(THERE, chunk),
            in_specs=[SCALARS, WHOLE] + [pl.BlockSpec(memory_space=pl.ANY)] * len(order),
            out_specs=[WHOLE] * len(shapes(THERE, chunk)),
            compiler_params=PARAMS,
            cost_estimate=cost(OTHER_BYTES),
            name="blur_y",
        )(psf, estimate, *order)
    moved = [exchange(parts, THERE, chunk) for chunk, parts in enumerate(sent)]

    seen = jnp.roll(measured[0], -offsets[0] * BLOCK, axis=2)
    seen = lax.cond(mirrors[0, 1] == 1, lambda arr: jnp.flip(arr, 2), lambda arr: arr, seen)
    seen = lax.cond(mirrors[0, 0] == 1, lambda arr: jnp.flip(arr, 0), lambda arr: arr, seen)

    spread = [None] * CHUNKS
    for chunk in reversed(range(CHUNKS)):
        spread[chunk] = pl.pallas_call(
            functools.partial(ratio_kernel, chunk),
            out_shape=shapes(BACK, chunk),
            in_specs=[SCALARS, SCALARS, SCALARS] + [WHOLE] * (1 + len(moved[chunk])),
            out_specs=[WHOLE] * len(shapes(BACK, chunk)),
            scratch_shapes=[
                pltpu.VMEM((depth, step, width), jnp.float32),
                pltpu.VMEM((depth, step, width), jnp.float32),
                pltpu.VMEM((depth * step, width + 2 * LANES), jnp.bfloat16),
                pltpu.VMEM((depth * step, width + 2 * LANES), jnp.bfloat16),
            ],
            compiler_params=PARAMS,
            cost_estimate=cost(RATIO_BYTES),
            name="ratio",
        )(offsets, mirrors, psf, seen, *moved[chunk])
        seen, _ = lax.optimization_barrier((seen, spread[chunk][0]))
    own, other = [], []
    for chunk in range(CHUNKS):
        returned = exchange(spread[chunk], BACK, chunk)
        own += returned
        if BACK[chunk] == "hl":
            swapped = lax.ppermute(jnp.concatenate(returned[1:]), "view", swap)
            other.append(lax.ppermute(returned[0], "view", swap))
            other += jnp.split(swapped, len(returned) - 1)
        else:
            other += [lax.ppermute(part, "view", swap) for part in returned]
    late_psf, _ = lax.optimization_barrier((psf, own[0]))
    other_psf = lax.ppermute(late_psf, "view", swap)

    def multiply(psf, factor, messages):
        return pl.pallas_call(
            product_kernel,
            out_shape=jax.ShapeDtypeStruct(estimate.shape, jnp.float32),
            in_specs=[SCALARS] + [WHOLE] * (1 + len(messages)),
            out_specs=WHOLE,
            scratch_shapes=[pltpu.VMEM((CHUNKS, slabs, step, width), jnp.float32)],
            compiler_params=PARAMS,
            cost_estimate=cost(OTHER_BYTES),
            name="product",
        )(psf, factor, *messages)

    return multiply(other_psf, multiply(psf, estimate, own), other)


def solution(mesh):
    placed = (
        P("slab", None, None),
        P("view", None, "slab", None),
        P("view"),
        P("view", None),
        P("view", None, None),
    )
    return jax.shard_map(
        body, mesh=mesh, in_specs=placed, out_specs=P("slab", None, None), check_vma=False
    )
```

time: 215 us -> 83.4 us (0.39)
  other arithmetic: 85.9 us -> 0.82 us
  blocking collectives: 68.8 us -> 0 us
  starting transfers between devices: 4 us -> 37.4 us
  Pallas kernels: 0 us -> 13.2 us
  between operations: 15.5 us -> 2.36 us
  waiting for transfers between devices: 34.1 us -> 23 us
    all_to_all x2 -> x0, blocking collectives: 68.8 us -> none  [the longest x1 36.8 us: body(): lax.all_to_all(jnp.stack(corrections), 'slab', split_axis=1, concat_axis=...]
    add x5 -> x0, other arithmetic: 66.6 us -> none  [convolve(): summed + tap_row[tap_index] * lax.slice_in_dim(volume, tap_index, tap_ind...]
    all_gather x1 -> x0, waiting for transfers between devices: 34.1 us -> none  [body(): gathered = lax.all_gather(local_product[None], 'view', axis=0, tiled=True)]
    ppermute x2 -> x31, starting transfers between devices: 4 us -> 37.4 us  [the longest x24 29.6 us: send(): lax.ppermute(part, 'slab', [(i, i ^ k * unit) for i in range(slabs)])]
    ppermute x2 -> x31, waiting for transfers between devices: 0.01 us -> 23 us  [the longest x24 15.1 us: send(): lax.ppermute(part, 'slab', [(i, i ^ k * unit) for i in range(slabs)])]
    div x1 -> x0, other arithmetic: 15.1 us -> none  [body(): ratio = measured[0] / blurred]
    pallas_call x0 -> x6, Pallas kernels: none -> 13.2 us  [the longest x2 6.95 us: body(): pl.pallas_call(functools.partial(ratio_kernel, chunk), out_shape=shapes(B...]
  transfers between devices with their start and end apart: 3 -> 31, of which waited for: 1 -> 12; matrix products, arithmetic and copies ran while one was open for 1% -> 6% of each run, Pallas kernels for 0% -> 12%
where the time goes in v1:
time: 83.4 us; the launch traced here: 83.2 us
  starting transfers between devices  37.4 us (45%)
  waiting for transfers between devices  23 us (28%)
  Pallas kernels  13.2 us (16%)
  local copies, waits for them, and re-layouts  6.31 us (8%)
  between operations  2.36 us (3%)
    ppermute x24, starting transfers between devices, send(): lax.ppermute(part, 'slab', [(i, i ^ k * unit) for i in range(slabs)])  29.6 us
    ppermute x24, waiting for transfers between devices, send(): lax.ppermute(part, 'slab', [(i, i ^ k * unit) for i in range(slabs)])  15.1 us
    ppermute x4, waiting for transfers between devices, body(): other += [lax.ppermute(part, 'view', swap) for part in returned]  7.17 us
    pallas_call x2, Pallas kernels, body(): pl.pallas_call(functools.partial(ratio_kernel, chunk), out_shape=shapes(B...  6.95 us
    ppermute x4, starting transfers between devices, body(): other += [lax.ppermute(part, 'view', swap) for part in returned]  4.52 us
    pallas_call x2, Pallas kernels, multiply(): pl.pallas_call(product_kernel, out_shape=jax.ShapeDtypeStruct(estimate.sh...  3.98 us
    slice x16, local copies, waits for them, and re-layouts, exchange(): part[at]  2.4 us
    pallas_call x2, Pallas kernels, body(): pl.pallas_call(functools.partial(blur_y_kernel, chunk), out_shape=shapes(...  2.29 us
  transfers between devices with their start and end apart: 31, of which 12 were waited for; matrix products, arithmetic and copies ran while one was open for 6% of the time, Pallas kernels for 12%

profile of v1, /device:TPU:0, one launch (start us, length us, event | category | flops | bytes accessed | tf_op | source)
XLA Modules:
  0.0 83.2 jit_solution(6882434197724902756)
XLA Ops:
  0.0 0.7 copy.9.psf_ref
  0.7 1.2 %copy-done = f32[1,256,1024]{2,1,0:T(8,128)S(1)} copy-done((f32[1,256,1024]{2,1,0:T(8,128)S(1)}, f32[1,256,1024]{2,1,0:T(8,128)}, u32[]{:S(2)}) %copy-start) | copy-done | bytes 1048600
  1.9 1.1 %blur_y.2 = (f32[4,8,1024]{2,1,0:T(8,128)S(1)}, f32[4,8,1024]{2,1,0:T(8,128)S(1)}, f32[4,8,1024]{2,1,0:T(8,128)S(1)}, f32[4,8,1024]{2,1,0:T(8,128)S(1)}) custom-call(f32[1,3,17]{2,1,0:T(4,128)S(1)} %copy.9.psf_ref, f32[1,256,1024]{2,1,0:T(8,128)S(1)} %copy-done), custom_call_target="tpu_custom_call" | custom-call | bytes 6291456 | tf_op jit(solution)/shard_map/blur_y/pallas_call | solution.py:296
  3.1 3.1 %collective-permute-start = (f32[4,8,1024]{2,1,0:T(8,128)S(1)}, f32[4,8,1024]{2,1,0:T(8,128)}, u32[]{:S(2)}, u32[]{:S(2)}) collective-permute-start(f32[4,8,1024]{2,1,0:T(8,128)S(1)} %get-tuple-element.34), channel_id=1, source_target_pairs={{0,4},{1,5},{2,6},{3,7},{4,0},{5,1},{6,2},{7,3},{8,12},{9,13},{10,... | collective-permute-start | bytes 393224 | tf_op jit(solution)/shard_map/ppermute | solution.py:284
  6.2 2.6 %collective-permute-start.1 = (f32[4,8,1024]{2,1,0:T(8,128)S(1)}, f32[4,8,1024]{2,1,0:T(8,128)}, u32[]{:S(2)}, u32[]{:S(2)}) collective-permute-start(f32[4,8,1024]{2,1,0:T(8,128)S(1)} %get-tuple-element.35), channel_id=1, source_target_pairs={{0,8},{1,9},{2,10},{3,11},{4,12},{5,13},{6,14},{7,15},{8,0},{9,1},... | collective-permute-start | bytes 393224 | tf_op jit(solution)/shard_map/ppermute | solution.py:284
  8.7 1.1 %blur_y.3 = (f32[4,8,1024]{2,1,0:T(8,128)S(1)}, f32[4,8,1024]{2,1,0:T(8,128)S(1)}, f32[4,8,1024]{2,1,0:T(8,128)S(1)}, f32[4,8,1024]{2,1,0:T(8,128)S(1)}) custom-call(f32[1,3,17]{2,1,0:T(4,128)S(1)} %copy.9.psf_ref, f32[1,256,1024]{2,1,0:T(8,128)S(1)} %copy-done, f32[4,8,1024]{2,1,0:T(8,128)S(1)} %get-tuple-element.33.refs_0_), custom_call_target="tpu_custom_call" | custom-call | bytes 6291456 | tf_op jit(solution)/shard_map/blur_y/pallas_call | solution.py:296
  9.9 0.1 collective-permute-start.6
  10.0 1.8 %collective-permute-start.7 = (f32[4,8,1024]{2,1,0:T(8,128)S(1)}, f32[4,8,1024]{2,1,0:T(8,128)S(1)}, u32[]{:S(2)}, u32[]{:S(2)}) collective-permute-start(f32[4,8,1024]{2,1,0:T(8,128)S(1)} %get-tuple-element.41), channel_id=1, source_target_pairs={{0,2},{1,3},{2,0},{3,1},{4,6},{5,7},{6,4},{7,5},{8,10},{9,11},{10,... | collective-permute-start | bytes 393224 | tf_op jit(solution)/shard_map/ppermute | solution.py:284
  12.4 0.6 fusion.14
  13.1 0.6 fusion.18
  14.9 0.6 fusion
  15.6 1.1 %conditional.2 = (f32[16,16,1024]{2,1,0:T(8,128)S(1)}) conditional(s32[]{:T(128)} %bitcast.1, f32[16,16,1024]{2,1,0:T(8,128)S(1)} %fusion, f32[16,16,1024]{2,1,0:T(8,128)S(1)} %fusion), branch_computations={%region_0.1_spmd, %region_1.2_spmd} | conditional | bytes 4194312 | solution.py:308
  15.6 0.1 copy.19
  15.7 1.0 %rev.6 = f32[16,16,1024]{2,1,0:T(8,128)S(1)} reverse(f32[16,16,1024]{2,1,0:T(8,128)S(1)} %copy.19), dimensions={2} | reverse | bytes 2097152 | tf_op jit(solution)/shard_map/cond/branch_1_fun/jit(_flip)/rev | solution.py:308
  16.7 0.2 conditional.3
  16.7 0.1 copy.20
  16.8 0.1 rev.7
  16.9 0.0 copy-start.5
  17.0 0.2 collective-permute-start.8
  17.1 0.8 fusion.15
  18.0 1.2 %collective-permute-done.1 = f32[4,8,1024]{2,1,0:T(8,128)} collective-permute-done((f32[4,8,1024]{2,1,0:T(8,128)S(1)}, f32[4,8,1024]{2,1,0:T(8,128)}, u32[]{:S(2)}, u32[]{:S(2)}) %collective-permute-start.1) | collective-permute-done | bytes 131104 | tf_op jit(solution)/shard_map/ppermute | solution.py:284
  19.2 0.8 fusion.16
  20.1 0.1 collective-permute-start.3
  20.2 1.6 %collective-permute-start.4 = (f32[4,8,1024]{2,1,0:T(8,128)S(1)}, f32[4,8,1024]{2,1,0:T(8,128)S(1)}, u32[]{:S(2)}, u32[]{:S(2)}) collective-permute-start(f32[4,8,1024]{2,1,0:T(8,128)S(1)} %pad_maximum_fusion.3), channel_id=1, source_target_pairs={{0,2},{1,3},{2,0},{3,1},{4,6},{5,7},{6,4},{7,5},{8,10},{9,11},{10,... | collective-permute-start | bytes 393224 | tf_op jit(solution)/shard_map/ppermute | solution.py:284
  21.8 0.4 collective-permute-start.5
  22.2 0.3 collective-permute-done.8
  22.5 1.8 %collective-permute-start.10 = (f32[4,8,1024]{2,1,0:T(8,128)S(1)}, f32[4,8,1024]{2,1,0:T(8,128)S(1)}, u32[]{:S(2)}, u32[]{:S(2)}) collective-permute-start(f32[4,8,1024]{2,1,0:T(8,128)S(1)} %pad_maximum_fusion.7), channel_id=1, source_target_pairs={{0,8},{1,9},{2,10},{3,11},{4,12},{5,13},{6,14},{7,15},{8,0},{9,1},... | collective-permute-start | bytes 393224 | tf_op jit(solution)/shard_map/ppermute | solution.py:284
  24.4 1.9 %collective-permute-start.11 = (f32[4,8,1024]{2,1,0:T(8,128)S(1)}, f32[4,8,1024]{2,1,0:T(8,128)S(1)}, u32[]{:S(2)}, u32[]{:S(2)}) collective-permute-start(f32[4,8,1024]{2,1,0:T(8,128)S(1)} %pad_maximum_fusion.8), channel_id=1, source_target_pairs={{0,12},{1,13},{2,14},{3,15},{4,8},{5,9},{6,10},{7,11},{8,4},{9,5},... | collective-permute-start | bytes 393224 | tf_op jit(solution)/shard_map/ppermute | solution.py:284
  26.4 0.6 collective-permute-start.9
  27.0 1.5 %collective-permute-done.5.refs_3_ = f32[4,8,1024]{2,1,0:T(8,128)S(1)} collective-permute-done((f32[4,8,1024]{2,1,0:T(8,128)S(1)}, f32[4,8,1024]{2,1,0:T(8,128)S(1)}, u32[]{:S(2)}, u32[]{:S(2)}) %collective-permute-start.5) | collective-permute-done | bytes 131104 | tf_op jit(solution)/shard_map/ppermute | solution.py:284
  28.5 3.5 %ratio.2 = (f32[4,8,1024]{2,1,0:T(8,128)S(1)}, f32[4,8,1024]{2,1,0:T(8,128)S(1)}, f32[4,8,1024]{2,1,0:T(8,128)S(1)}, f32[4,8,1024]{2,1,0:T(8,128)S(1)}) custom-call(s32[1]{0:T(128)S(6)} %copy.18.offset_ref, s32[1,2]{1,0:T(1,128)S(1)} %copy-done.2, f32[1,3,17]{2,1,0:T(4,128)S(1)} %copy.9.psf_ref, f32[16,16,1024]{2,1,0:T(8,128)S(1)} %get-tuple-element.121.meas_ref, ...), custom_call_target="tpu_custom_call" | custom-call | bytes 12582912 | tf_op jit(solution)/shard_map/ratio/pallas_call | solution.py:313
  32.0 1.1 %collective-permute-start.19 = (f32[4,8,1024]{2,1,0:T(8,128)S(1)}, f32[4,8,1024]{2,1,0:T(8,128)S(1)}, u32[]{:S(2)}, u32[]{:S(2)}) collective-permute-start(f32[4,8,1024]{2,1,0:T(8,128)S(1)} %get-tuple-element.48), channel_id=1, source_target_pairs={{0,4},{1,5},{2,6},{3,7},{4,0},{5,1},{6,2},{7,3},{8,12},{9,13},{10,... | collective-permute-start | bytes 393224 | tf_op jit(solution)/shard_map/ppermute | solution.py:284
  33.1 2.7 %collective-permute-start.20 = (f32[4,8,1024]{2,1,0:T(8,128)S(1)}, f32[4,8,1024]{2,1,0:T(8,128)S(1)}, u32[]{:S(2)}, u32[]{:S(2)}) collective-permute-start(f32[4,8,1024]{2,1,0:T(8,128)S(1)} %get-tuple-element.49), channel_id=1, source_target_pairs={{0,8},{1,9},{2,10},{3,11},{4,12},{5,13},{6,14},{7,15},{8,0},{9,1},... | collective-permute-start | bytes 393224 | tf_op jit(solution)/shard_map/ppermute | solution.py:284
  35.9 1.8 %collective-permute-start.21 = (f32[4,8,1024]{2,1,0:T(8,128)S(1)}, f32[4,8,1024]{2,1,0:T(8,128)S(1)}, u32[]{:S(2)}, u32[]{:S(2)}) collective-permute-start(f32[4,8,1024]{2,1,0:T(8,128)S(1)} %get-tuple-element.50), channel_id=1, source_target_pairs={{0,12},{1,13},{2,14},{3,15},{4,8},{5,9},{6,10},{7,11},{8,4},{9,5},... | collective-permute-start | bytes 393224 | tf_op jit(solution)/shard_map/ppermute | solution.py:284
  37.6 3.5 %ratio.3 = (f32[4,8,1024]{2,1,0:T(8,128)S(1)}, f32[4,8,1024]{2,1,0:T(8,128)S(1)}, f32[4,8,1024]{2,1,0:T(8,128)S(1)}, f32[4,8,1024]{2,1,0:T(8,128)S(1)}) custom-call(s32[1]{0:T(128)S(6)} %copy.18.offset_ref, s32[1,2]{1,0:T(1,128)S(1)} %copy-done.2, f32[1,3,17]{2,1,0:T(4,128)S(1)} %copy.9.psf_ref, f32[16,16,1024]{2,1,0:T(8,128)S(1)} %get-tuple-element.121.meas_ref, ...), custom_call_target="tpu_custom_call" | custom-call | bytes 12582912 | tf_op jit(solution)/shard_map/ratio/pallas_call | solution.py:313
  41.1 0.1 collective-permute-start.12
  41.2 1.6 %collective-permute-start.13 = (f32[4,8,1024]{2,1,0:T(8,128)S(1)}, f32[4,8,1024]{2,1,0:T(8,128)S(1)}, u32[]{:S(2)}, u32[]{:S(2)}) collective-permute-start(f32[4,8,1024]{2,1,0:T(8,128)S(1)} %get-tuple-element.45), channel_id=1, source_target_pairs={{0,2},{1,3},{2,0},{3,1},{4,6},{5,7},{6,4},{7,5},{8,10},{9,11},{10,... | collective-permute-start | bytes 393224 | tf_op jit(solution)/shard_map/ppermute | solution.py:284
  42.8 0.3 collective-permute-start.14
  43.1 3.5 %collective-permute-done.20 = f32[4,8,1024]{2,1,0:T(8,128)S(1)} collective-permute-done((f32[4,8,1024]{2,1,0:T(8,128)S(1)}, f32[4,8,1024]{2,1,0:T(8,128)S(1)}, u32[]{:S(2)}, u32[]{:S(2)}) %collective-permute-start.20) | collective-permute-done | bytes 131104 | tf_op jit(solution)/shard_map/ppermute | solution.py:284
  46.7 0.1 collective-permute-start.24
  46.8 1.3 %collective-permute-start.23 = (f32[4,8,1024]{2,1,0:T(8,128)S(1)}, f32[4,8,1024]{2,1,0:T(8,128)S(1)}, u32[]{:S(2)}, u32[]{:S(2)}) collective-permute-start(f32[4,8,1024]{2,1,0:T(8,128)S(1)} %pad_maximum_fusion.15), channel_id=1, source_target_pairs={{0,2},{1,3},{2,0},{3,1},{4,6},{5,7},{6,4},{7,5},{8,10},{9,11},{10,... | collective-permute-start | bytes 393224 | tf_op jit(solution)/shard_map/ppermute | solution.py:284
  48.1 0.6 collective-permute-start.22
  48.8 0.0 copy-start.8
  48.8 0.6 collective-permute-done.14
  49.5 0.0 copy-start.1
  49.5 2.3 %collective-permute-start.18 = (f32[4,8,1024]{2,1,0:T(8,128)S(1)}, f32[4,8,1024]{2,1,0:T(8,128)S(1)}, u32[]{:S(2)}, u32[]{:S(2)}) collective-permute-start(f32[4,8,1024]{2,1,0:T(8,128)S(1)} %pad_maximum_fusion.12), channel_id=1, source_target_pairs={{0,12},{1,13},{2,14},{3,15},{4,8},{5,9},{6,10},{7,11},{8,4},{9,5},... | collective-permute-start | bytes 393224 | tf_op jit(solution)/shard_map/ppermute | solution.py:284
  51.8 0.8 collective-permute-done.24.refs_7_
  52.6 2.9 %collective-permute-done.23.refs_6_ = f32[4,8,1024]{2,1,0:T(8,128)S(1)} collective-permute-done((f32[4,8,1024]{2,1,0:T(8,128)S(1)}, f32[4,8,1024]{2,1,0:T(8,128)S(1)}, u32[]{:S(2)}, u32[]{:S(2)}) %collective-permute-start.23) | collective-permute-done | bytes 131104 | tf_op jit(solution)/shard_map/ppermute | solution.py:284
  55.5 1.6 %collective-permute-start.30 = (f32[12,8,1024]{2,1,0:T(8,128)S(1)}, f32[12,8,1024]{2,1,0:T(8,128)S(1)}, u32[]{:S(2)}, u32[]{:S(2)}) collective-permute-start(f32[12,8,1024]{2,1,0:T(8,128)S(1)} %pad_maximum_fusion), channel_id=1, source_target_pairs={{0,16},{16,0},{1,17},{17,1},{2,18},{18,2},{3,19},{19,3},{4,20},{20... | collective-permute-start | bytes 1179656 | tf_op jit(solution)/shard_map/ppermute | solution.py:334
  57.2 3.5 %collective-permute-start.17 = (f32[4,8,1024]{2,1,0:T(8,128)S(1)}, f32[4,8,1024]{2,1,0:T(8,128)S(1)}, u32[]{:S(2)}, u32[]{:S(2)}) collective-permute-start(f32[4,8,1024]{2,1,0:T(8,128)S(1)} %pad_maximum_fusion.11), channel_id=1, source_target_pairs={{0,8},{1,9},{2,10},{3,11},{4,12},{5,13},{6,14},{7,15},{8,0},{9,1},... | collective-permute-start | bytes 393224 | tf_op jit(solution)/shard_map/ppermute | solution.py:284
  60.6 0.1 collective-permute-start.16
  60.7 1.1 %collective-permute-start.25 = (f32[4,8,1024]{2,1,0:T(8,128)S(1)}, f32[4,8,1024]{2,1,0:T(8,128)S(1)}, u32[]{:S(2)}, u32[]{:S(2)}) collective-permute-start(f32[4,8,1024]{2,1,0:T(8,128)S(1)} %pad_maximum_fusion.9.refs_0_), channel_id=1, source_target_pairs={{0,16},{16,0},{1,17},{17,1},{2,18},{18,2},{3,19},{19,3},{4,20},{20... | collective-permute-start | bytes 393224 | tf_op jit(solution)/shard_map/ppermute | solution.py:338
  61.8 1.1 %collective-permute-start.15 = (f32[1,3,17]{2,1,0:T(4,128)S(1)}, f32[1,3,17]{2,1,0:T(4,128)S(1)}, u32[]{:S(2)}, u32[]{:S(2)}) collective-permute-start(f32[1,3,17]{2,1,0:T(4,128)S(1)} %copy.10), channel_id=1, source_target_pairs={{0,16},{16,0},{1,17},{17,1},{2,18},{18,2},{3,19},{19,3},{4,20},{20... | collective-permute-start | bytes 620 | tf_op jit(solution)/shard_map/ppermute | solution.py:340
  62.9 4.2 %collective-permute-done.17.refs_2_ = f32[4,8,1024]{2,1,0:T(8,128)S(1)} collective-permute-done((f32[4,8,1024]{2,1,0:T(8,128)S(1)}, f32[4,8,1024]{2,1,0:T(8,128)S(1)}, u32[]{:S(2)}, u32[]{:S(2)}) %collective-permute-start.17) | collective-permute-done | bytes 131104 | tf_op jit(solution)/shard_map/ppermute | solution.py:284
  67.1 0.6 collective-permute-start.29
  67.8 1.4 %collective-permute-start.28 = (f32[4,8,1024]{2,1,0:T(8,128)S(1)}, f32[4,8,1024]{2,1,0:T(8,128)S(1)}, u32[]{:S(2)}, u32[]{:S(2)}) collective-permute-start(f32[4,8,1024]{2,1,0:T(8,128)S(1)} %collective-permute-done.18.refs_3_), channel_id=1, source_target_pairs={{0,16},{16,0},{1,17},{17,1},{2,18},{18,2},{3,19},{19,3},{4,20},{20... | collective-permute-start | bytes 393224 | tf_op jit(solution)/shard_map/ppermute | solution.py:338
  69.1 1.5 %product.2.factor_ref = f32[1,256,1024]{2,1,0:T(8,128)S(1)} custom-call(f32[1,3,17]{2,1,0:T(4,128)S(1)} %copy.9.psf_ref, f32[1,256,1024]{2,1,0:T(8,128)S(1)} %copy-done.1, f32[4,8,1024]{2,1,0:T(8,128)S(1)} %pad_maximum_fusion.9.refs_0_, f32[4,8,1024]{2,1,0:T(8,128)S(1)} %collective-permute-done.16.refs_1_, ...), custom_call_target="tpu_custom_call" | custom-call | bytes 6291456 | tf_op jit(solution)/shard_map/product/pallas_call | solution.py:343
  70.7 1.3 %collective-permute-start.27 = (f32[4,8,1024]{2,1,0:T(8,128)S(1)}, f32[4,8,1024]{2,1,0:T(8,128)S(1)}, u32[]{:S(2)}, u32[]{:S(2)}) collective-permute-start(f32[4,8,1024]{2,1,0:T(8,128)S(1)} %collective-permute-done.17.refs_2_), channel_id=1, source_target_pairs={{0,16},{16,0},{1,17},{17,1},{2,18},{18,2},{3,19},{19,3},{4,20},{20... | collective-permute-start | bytes 393224 | tf_op jit(solution)/shard_map/ppermute | solution.py:338
  72.0 0.8 collective-permute-start.26
  72.8 0.8 collective-permute-done.29.refs_4_
  73.6 2.8 %collective-permute-done.28.refs_3_ = f32[4,8,1024]{2,1,0:T(8,128)S(1)} collective-permute-done((f32[4,8,1024]{2,1,0:T(8,128)S(1)}, f32[4,8,1024]{2,1,0:T(8,128)S(1)}, u32[]{:S(2)}, u32[]{:S(2)}) %collective-permute-start.28) | collective-permute-done | bytes 131104 | tf_op jit(solution)/shard_map/ppermute | solution.py:338
  76.4 2.8 %collective-permute-done.27.refs_2_ = f32[4,8,1024]{2,1,0:T(8,128)S(1)} collective-permute-done((f32[4,8,1024]{2,1,0:T(8,128)S(1)}, f32[4,8,1024]{2,1,0:T(8,128)S(1)}, u32[]{:S(2)}, u32[]{:S(2)}) %collective-permute-start.27) | collective-permute-done | bytes 131104 | tf_op jit(solution)/shard_map/ppermute | solution.py:338
  79.2 1.6 %collective-permute-done.26.refs_1_ = f32[4,8,1024]{2,1,0:T(8,128)S(1)} collective-permute-done((f32[4,8,1024]{2,1,0:T(8,128)S(1)}, f32[4,8,1024]{2,1,0:T(8,128)S(1)}, u32[]{:S(2)}, u32[]{:S(2)}) %collective-permute-start.26) | collective-permute-done | bytes 131104 | tf_op jit(solution)/shard_map/ppermute | solution.py:338
  80.7 2.5 %product.3 = f32[1,256,1024]{2,1,0:T(8,128)} custom-call(f32[1,3,17]{2,1,0:T(4,128)S(1)} %collective-permute-done.15.psf_ref, f32[1,256,1024]{2,1,0:T(8,128)S(1)} %product.2.factor_ref, f32[4,8,1024]{2,1,0:T(8,128)S(1)} %collective-permute-done.25.refs_0_, f32[4,8,1024]{2,1,0:T(8,128)S(1)} %collective-permute-done.26.refs_1_, ...), custom_call_target="tpu_custom_call" | custom-call | bytes 6291456 | tf_op jit(solution)/shard_map/product/pallas_call | solution.py:343
  (66 shorter events, 0.4 us)
Async XLA Ops:
  0.7 1.2 %copy-start = (f32[1,256,1024]{2,1,0:T(8,128)S(1)}, f32[1,256,1024]{2,1,0:T(8,128)}, u32[]{:S(2)}) copy-start(f32[1,256,1024]{2,1,0:T(8,128)} %factor_ref.1) | copy-start | bytes 3145732
  1.9 11.1 %copy-start.2 = (s32[1,2]{1,0:T(1,128)S(1)}, s32[1,2]{1,0:T(1,128)}, u32[]{:S(2)}) copy-start(s32[1,2]{1,0:T(1,128)} %mirror_ref.3) | copy-start | bytes 28
  1.9 13.0 %copy-start.3 = (f32[1,16,16,1024]{3,2,1,0:T(8,128)S(1)}, f32[1,16,16,1024]{3,2,1,0:T(8,128)}, u32[]{:S(2)}) copy-start(f32[1,16,16,1024]{3,2,1,0:T(8,128)} %param.10) | copy-start | bytes 3145732
  3.1 13.9 %collective-permute-start = (f32[4,8,1024]{2,1,0:T(8,128)S(1)}, f32[4,8,1024]{2,1,0:T(8,128)}, u32[]{:S(2)}, u32[]{:S(2)}) collective-permute-start(f32[4,8,1024]{2,1,0:T(8,128)S(1)} %get-tuple-element.34), channel_id=1, source_target_pairs={{0,4},{1,5},{2,6},{3,7},{4,0},{5,1},{6,2},{7,3},{8,12},{9,13},{10,... | collective-permute-start | bytes 393224 | tf_op jit(solution)/shard_map/ppermute | solution.py:284
  6.2 13.0 %collective-permute-start.1 = (f32[4,8,1024]{2,1,0:T(8,128)S(1)}, f32[4,8,1024]{2,1,0:T(8,128)}, u32[]{:S(2)}, u32[]{:S(2)}) collective-permute-start(f32[4,8,1024]{2,1,0:T(8,128)S(1)} %get-tuple-element.35), channel_id=1, source_target_pairs={{0,8},{1,9},{2,10},{3,11},{4,12},{5,13},{6,14},{7,15},{8,0},{9,1},... | collective-permute-start | bytes 393224 | tf_op jit(solution)/shard_map/ppermute | solution.py:284
  8.7 11.3 %collective-permute-start.2 = (f32[4,8,1024]{2,1,0:T(8,128)S(1)}, f32[4,8,1024]{2,1,0:T(8,128)S(1)}, u32[]{:S(2)}, u32[]{:S(2)}) collective-permute-start(f32[4,8,1024]{2,1,0:T(8,128)S(1)} %get-tuple-element.36), channel_id=1, source_target_pairs={{0,12},{1,13},{2,14},{3,15},{4,8},{5,9},{6,10},{7,11},{8,4},{9,5},... | collective-permute-start | bytes 393224 | tf_op jit(solution)/shard_map/ppermute | solution.py:284
  9.9 11.9 %collective-permute-start.6 = (f32[4,8,1024]{2,1,0:T(8,128)S(1)}, f32[4,8,1024]{2,1,0:T(8,128)S(1)}, u32[]{:S(2)}, u32[]{:S(2)}) collective-permute-start(f32[4,8,1024]{2,1,0:T(8,128)S(1)} %get-tuple-element.40), channel_id=1, source_target_pairs={{0,1},{1,0},{2,3},{3,2},{4,5},{5,4},{6,7},{7,6},{8,9},{9,8},{10,11... | collective-permute-start | bytes 393224 | tf_op jit(solution)/shard_map/ppermute | solution.py:284
  10.0 12.2 %collective-permute-start.7 = (f32[4,8,1024]{2,1,0:T(8,128)S(1)}, f32[4,8,1024]{2,1,0:T(8,128)S(1)}, u32[]{:S(2)}, u32[]{:S(2)}) collective-permute-start(f32[4,8,1024]{2,1,0:T(8,128)S(1)} %get-tuple-element.41), channel_id=1, source_target_pairs={{0,2},{1,3},{2,0},{3,1},{4,6},{5,7},{6,4},{7,5},{8,10},{9,11},{10,... | collective-permute-start | bytes 393224 | tf_op jit(solution)/shard_map/ppermute | solution.py:284
  16.9 3.1 %copy-start.7 = (f32[1,8,1024]{2,1,0:T(8,128)S(1)}, f32[1,8,1024]{2,1,0:T(8,128)}, u32[]{:S(2)}) copy-start(f32[1,8,1024]{2,1,0:T(8,128)} %get-tuple-element.104) | copy-start | bytes 98308
  16.9 3.2 %copy-start.6 = (f32[1,8,1024]{2,1,0:T(8,128)S(1)}, f32[1,8,1024]{2,1,0:T(8,128)}, u32[]{:S(2)}) copy-start(f32[1,8,1024]{2,1,0:T(8,128)} %get-tuple-element.103) | copy-start | bytes 98308
  16.9 4.8 %copy-start.5 = (f32[1,8,1024]{2,1,0:T(8,128)S(1)}, f32[1,8,1024]{2,1,0:T(8,128)}, u32[]{:S(2)}) copy-start(f32[1,8,1024]{2,1,0:T(8,128)} %get-tuple-element.102) | copy-start | bytes 98308
  17.0 5.5 %collective-permute-start.8 = (f32[4,8,1024]{2,1,0:T(8,128)S(1)}, f32[4,8,1024]{2,1,0:T(8,128)S(1)}, u32[]{:S(2)}, u32[]{:S(2)}) collective-permute-start(f32[4,8,1024]{2,1,0:T(8,128)S(1)} %get-tuple-element.42), channel_id=1, source_target_pairs={{0,3},{1,2},{2,1},{3,0},{4,7},{5,6},{6,5},{7,4},{8,11},{9,10},{10,... | collective-permute-start | bytes 393224 | tf_op jit(solution)/shard_map/ppermute | solution.py:284
  20.0 6.3 %copy-start.4 = (f32[1,8,1024]{2,1,0:T(8,128)S(1)}, f32[1,8,1024]{2,1,0:T(8,128)}, u32[]{:S(2)}) copy-start(f32[1,8,1024]{2,1,0:T(8,128)} %get-tuple-element.105) | copy-start | bytes 98308
  20.1 6.3 %collective-permute-start.3 = (f32[4,8,1024]{2,1,0:T(8,128)S(1)}, f32[4,8,1024]{2,1,0:T(8,128)S(1)}, u32[]{:S(2)}, u32[]{:S(2)}) collective-permute-start(f32[4,8,1024]{2,1,0:T(8,128)S(1)} %pad_maximum_fusion.2), channel_id=1, source_target_pairs={{0,1},{1,0},{2,3},{3,2},{4,5},{5,4},{6,7},{7,6},{8,9},{9,8},{10,11... | collective-permute-start | bytes 393224 | tf_op jit(solution)/shard_map/ppermute | solution.py:284
  20.2 6.8 %collective-permute-start.4 = (f32[4,8,1024]{2,1,0:T(8,128)S(1)}, f32[4,8,1024]{2,1,0:T(8,128)S(1)}, u32[]{:S(2)}, u32[]{:S(2)}) collective-permute-start(f32[4,8,1024]{2,1,0:T(8,128)S(1)} %pad_maximum_fusion.3), channel_id=1, source_target_pairs={{0,2},{1,3},{2,0},{3,1},{4,6},{5,7},{6,4},{7,5},{8,10},{9,11},{10,... | collective-permute-start | bytes 393224 | tf_op jit(solution)/shard_map/ppermute | solution.py:284
  21.8 6.8 %collective-permute-start.5 = (f32[4,8,1024]{2,1,0:T(8,128)S(1)}, f32[4,8,1024]{2,1,0:T(8,128)S(1)}, u32[]{:S(2)}, u32[]{:S(2)}) collective-permute-start(f32[4,8,1024]{2,1,0:T(8,128)S(1)} %pad_maximum_fusion.4), channel_id=1, source_target_pairs={{0,3},{1,2},{2,1},{3,0},{4,7},{5,6},{6,5},{7,4},{8,11},{9,10},{10,... | collective-permute-start | bytes 393224 | tf_op jit(solution)/shard_map/ppermute | solution.py:284
  22.5 13.3 %collective-permute-start.10 = (f32[4,8,1024]{2,1,0:T(8,128)S(1)}, f32[4,8,1024]{2,1,0:T(8,128)S(1)}, u32[]{:S(2)}, u32[]{:S(2)}) collective-permute-start(f32[4,8,1024]{2,1,0:T(8,128)S(1)} %pad_maximum_fusion.7), channel_id=1, source_target_pairs={{0,8},{1,9},{2,10},{3,11},{4,12},{5,13},{6,14},{7,15},{8,0},{9,1},... | collective-permute-start | bytes 393224 | tf_op jit(solution)/shard_map/ppermute | solution.py:284
  24.4 13.2 %collective-permute-start.11 = (f32[4,8,1024]{2,1,0:T(8,128)S(1)}, f32[4,8,1024]{2,1,0:T(8,128)S(1)}, u32[]{:S(2)}, u32[]{:S(2)}) collective-permute-start(f32[4,8,1024]{2,1,0:T(8,128)S(1)} %pad_maximum_fusion.8), channel_id=1, source_target_pairs={{0,12},{1,13},{2,14},{3,15},{4,8},{5,9},{6,10},{7,11},{8,4},{9,5},... | collective-permute-start | bytes 393224 | tf_op jit(solution)/shard_map/ppermute | solution.py:284
  26.4 11.2 %collective-permute-start.9 = (f32[4,8,1024]{2,1,0:T(8,128)S(1)}, f32[4,8,1024]{2,1,0:T(8,128)S(1)}, u32[]{:S(2)}, u32[]{:S(2)}) collective-permute-start(f32[4,8,1024]{2,1,0:T(8,128)S(1)} %pad_maximum_fusion.6), channel_id=1, source_target_pairs={{0,4},{1,5},{2,6},{3,7},{4,0},{5,1},{6,2},{7,3},{8,12},{9,13},{10,... | collective-permute-start | bytes 393224 | tf_op jit(solution)/shard_map/ppermute | solution.py:284
  32.0 10.8 %collective-permute-start.19 = (f32[4,8,1024]{2,1,0:T(8,128)S(1)}, f32[4,8,1024]{2,1,0:T(8,128)S(1)}, u32[]{:S(2)}, u32[]{:S(2)}) collective-permute-start(f32[4,8,1024]{2,1,0:T(8,128)S(1)} %get-tuple-element.48), channel_id=1, source_target_pairs={{0,4},{1,5},{2,6},{3,7},{4,0},{5,1},{6,2},{7,3},{8,12},{9,13},{10,... | collective-permute-start | bytes 393224 | tf_op jit(solution)/shard_map/ppermute | solution.py:284
  33.1 13.5 %collective-permute-start.20 = (f32[4,8,1024]{2,1,0:T(8,128)S(1)}, f32[4,8,1024]{2,1,0:T(8,128)S(1)}, u32[]{:S(2)}, u32[]{:S(2)}) collective-permute-start(f32[4,8,1024]{2,1,0:T(8,128)S(1)} %get-tuple-element.49), channel_id=1, source_target_pairs={{0,8},{1,9},{2,10},{3,11},{4,12},{5,13},{6,14},{7,15},{8,0},{9,1},... | collective-permute-start | bytes 393224 | tf_op jit(solution)/shard_map/ppermute | solution.py:284
  35.9 10.8 %collective-permute-start.21 = (f32[4,8,1024]{2,1,0:T(8,128)S(1)}, f32[4,8,1024]{2,1,0:T(8,128)S(1)}, u32[]{:S(2)}, u32[]{:S(2)}) collective-permute-start(f32[4,8,1024]{2,1,0:T(8,128)S(1)} %get-tuple-element.50), channel_id=1, source_target_pairs={{0,12},{1,13},{2,14},{3,15},{4,8},{5,9},{6,10},{7,11},{8,4},{9,5},... | collective-permute-start | bytes 393224 | tf_op jit(solution)/shard_map/ppermute | solution.py:284
  41.1 7.0 %collective-permute-start.12 = (f32[4,8,1024]{2,1,0:T(8,128)S(1)}, f32[4,8,1024]{2,1,0:T(8,128)S(1)}, u32[]{:S(2)}, u32[]{:S(2)}) collective-permute-start(f32[4,8,1024]{2,1,0:T(8,128)S(1)} %get-tuple-element.44), channel_id=1, source_target_pairs={{0,1},{1,0},{2,3},{3,2},{4,5},{5,4},{6,7},{7,6},{8,9},{9,8},{10,11... | collective-permute-start | bytes 393224 | tf_op jit(solution)/shard_map/ppermute | solution.py:284
  41.2 7.6 %collective-permute-start.13 = (f32[4,8,1024]{2,1,0:T(8,128)S(1)}, f32[4,8,1024]{2,1,0:T(8,128)S(1)}, u32[]{:S(2)}, u32[]{:S(2)}) collective-permute-start(f32[4,8,1024]{2,1,0:T(8,128)S(1)} %get-tuple-element.45), channel_id=1, source_target_pairs={{0,2},{1,3},{2,0},{3,1},{4,6},{5,7},{6,4},{7,5},{8,10},{9,11},{10,... | collective-permute-start | bytes 393224 | tf_op jit(solution)/shard_map/ppermute | solution.py:284
  42.8 6.6 %collective-permute-start.14 = (f32[4,8,1024]{2,1,0:T(8,128)S(1)}, f32[4,8,1024]{2,1,0:T(8,128)S(1)}, u32[]{:S(2)}, u32[]{:S(2)}) collective-permute-start(f32[4,8,1024]{2,1,0:T(8,128)S(1)} %get-tuple-element.46), channel_id=1, source_target_pairs={{0,3},{1,2},{2,1},{3,0},{4,7},{5,6},{6,5},{7,4},{8,11},{9,10},{10,... | collective-permute-start | bytes 393224 | tf_op jit(solution)/shard_map/ppermute | solution.py:284
  46.7 5.9 %collective-permute-start.24 = (f32[4,8,1024]{2,1,0:T(8,128)S(1)}, f32[4,8,1024]{2,1,0:T(8,128)S(1)}, u32[]{:S(2)}, u32[]{:S(2)}) collective-permute-start(f32[4,8,1024]{2,1,0:T(8,128)S(1)} %pad_maximum_fusion.16), channel_id=1, source_target_pairs={{0,3},{1,2},{2,1},{3,0},{4,7},{5,6},{6,5},{7,4},{8,11},{9,10},{10,... | collective-permute-start | bytes 393224 | tf_op jit(solution)/shard_map/ppermute | solution.py:284
  46.8 8.7 %collective-permute-start.23 = (f32[4,8,1024]{2,1,0:T(8,128)S(1)}, f32[4,8,1024]{2,1,0:T(8,128)S(1)}, u32[]{:S(2)}, u32[]{:S(2)}) collective-permute-start(f32[4,8,1024]{2,1,0:T(8,128)S(1)} %pad_maximum_fusion.15), channel_id=1, source_target_pairs={{0,2},{1,3},{2,0},{3,1},{4,6},{5,7},{6,4},{7,5},{8,10},{9,11},{10,... | collective-permute-start | bytes 393224 | tf_op jit(solution)/shard_map/ppermute | solution.py:284
  48.1 7.4 %collective-permute-start.22 = (f32[4,8,1024]{2,1,0:T(8,128)S(1)}, f32[4,8,1024]{2,1,0:T(8,128)S(1)}, u32[]{:S(2)}, u32[]{:S(2)}) collective-permute-start(f32[4,8,1024]{2,1,0:T(8,128)S(1)} %pad_maximum_fusion.14), channel_id=1, source_target_pairs={{0,1},{1,0},{2,3},{3,2},{4,5},{5,4},{6,7},{7,6},{8,9},{9,8},{10,11... | collective-permute-start | bytes 393224 | tf_op jit(solution)/shard_map/ppermute | solution.py:284
  48.8 13.0 %copy-start.8 = (f32[1,3,17]{2,0,1:T(1,128)S(1)}, f32[1,3,17]{2,0,1:T(1,128)}, u32[]{:S(2)}) copy-start(f32[1,3,17]{2,0,1:T(1,128)} %param.13) | copy-start | bytes 616
  49.5 19.7 %copy-start.1 = (f32[1,256,1024]{2,1,0:T(8,128)S(1)}, f32[1,256,1024]{2,1,0:T(8,128)}, u32[]{:S(2)}) copy-start(f32[1,256,1024]{2,1,0:T(8,128)} %factor_ref.1) | copy-start | bytes 3145732
  49.5 12.3 %collective-permute-start.18 = (f32[4,8,1024]{2,1,0:T(8,128)S(1)}, f32[4,8,1024]{2,1,0:T(8,128)S(1)}, u32[]{:S(2)}, u32[]{:S(2)}) collective-permute-start(f32[4,8,1024]{2,1,0:T(8,128)S(1)} %pad_maximum_fusion.12), channel_id=1, source_target_pairs={{0,12},{1,13},{2,14},{3,15},{4,8},{5,9},{6,10},{7,11},{8,4},{9,5},... | collective-permute-start | bytes 393224 | tf_op jit(solution)/shard_map/ppermute | solution.py:284
  55.5 16.5 %collective-permute-start.30 = (f32[12,8,1024]{2,1,0:T(8,128)S(1)}, f32[12,8,1024]{2,1,0:T(8,128)S(1)}, u32[]{:S(2)}, u32[]{:S(2)}) collective-permute-start(f32[12,8,1024]{2,1,0:T(8,128)S(1)} %pad_maximum_fusion), channel_id=1, source_target_pairs={{0,16},{16,0},{1,17},{17,1},{2,18},{18,2},{3,19},{19,3},{4,20},{20... | collective-permute-start | bytes 1179656 | tf_op jit(solution)/shard_map/ppermute | solution.py:334
  57.2 10.0 %collective-permute-start.17 = (f32[4,8,1024]{2,1,0:T(8,128)S(1)}, f32[4,8,1024]{2,1,0:T(8,128)S(1)}, u32[]{:S(2)}, u32[]{:S(2)}) collective-permute-start(f32[4,8,1024]{2,1,0:T(8,128)S(1)} %pad_maximum_fusion.11), channel_id=1, source_target_pairs={{0,8},{1,9},{2,10},{3,11},{4,12},{5,13},{6,14},{7,15},{8,0},{9,1},... | collective-permute-start | bytes 393224 | tf_op jit(solution)/shard_map/ppermute | solution.py:284
  60.6 7.1 %collective-permute-start.16 = (f32[4,8,1024]{2,1,0:T(8,128)S(1)}, f32[4,8,1024]{2,1,0:T(8,128)S(1)}, u32[]{:S(2)}, u32[]{:S(2)}) collective-permute-start(f32[4,8,1024]{2,1,0:T(8,128)S(1)} %pad_maximum_fusion.10), channel_id=1, source_target_pairs={{0,4},{1,5},{2,6},{3,7},{4,0},{5,1},{6,2},{7,3},{8,12},{9,13},{10,... | collective-permute-start | bytes 393224 | tf_op jit(solution)/shard_map/ppermute | solution.py:284
  60.7 12.8 %collective-permute-start.25 = (f32[4,8,1024]{2,1,0:T(8,128)S(1)}, f32[4,8,1024]{2,1,0:T(8,128)S(1)}, u32[]{:S(2)}, u32[]{:S(2)}) collective-permute-start(f32[4,8,1024]{2,1,0:T(8,128)S(1)} %pad_maximum_fusion.9.refs_0_), channel_id=1, source_target_pairs={{0,16},{16,0},{1,17},{17,1},{2,18},{18,2},{3,19},{19,3},{4,20},{20... | collective-permute-start | bytes 393224 | tf_op jit(solution)/shard_map/ppermute | solution.py:338
  61.8 8.9 %collective-permute-start.15 = (f32[1,3,17]{2,1,0:T(4,128)S(1)}, f32[1,3,17]{2,1,0:T(4,128)S(1)}, u32[]{:S(2)}, u32[]{:S(2)}) collective-permute-start(f32[1,3,17]{2,1,0:T(4,128)S(1)} %copy.10), channel_id=1, source_target_pairs={{0,16},{16,0},{1,17},{17,1},{2,18},{18,2},{3,19},{19,3},{4,20},{20... | collective-permute-start | bytes 620 | tf_op jit(solution)/shard_map/ppermute | solution.py:340
  67.1 6.4 %collective-permute-start.29 = (f32[4,8,1024]{2,1,0:T(8,128)S(1)}, f32[4,8,1024]{2,1,0:T(8,128)S(1)}, u32[]{:S(2)}, u32[]{:S(2)}) collective-permute-start(f32[4,8,1024]{2,1,0:T(8,128)S(1)} %pad_maximum_fusion.13.refs_4_), channel_id=1, source_target_pairs={{0,16},{16,0},{1,17},{17,1},{2,18},{18,2},{3,19},{19,3},{4,20},{20... | collective-permute-start | bytes 393224 | tf_op jit(solution)/shard_map/ppermute | solution.py:335
  67.8 8.6 %collective-permute-start.28 = (f32[4,8,1024]{2,1,0:T(8,128)S(1)}, f32[4,8,1024]{2,1,0:T(8,128)S(1)}, u32[]{:S(2)}, u32[]{:S(2)}) collective-permute-start(f32[4,8,1024]{2,1,0:T(8,128)S(1)} %collective-permute-done.18.refs_3_), channel_id=1, source_target_pairs={{0,16},{16,0},{1,17},{17,1},{2,18},{18,2},{3,19},{19,3},{4,20},{20... | collective-permute-start | bytes 393224 | tf_op jit(solution)/shard_map/ppermute | solution.py:338
  70.7 8.5 %collective-permute-start.27 = (f32[4,8,1024]{2,1,0:T(8,128)S(1)}, f32[4,8,1024]{2,1,0:T(8,128)S(1)}, u32[]{:S(2)}, u32[]{:S(2)}) collective-permute-start(f32[4,8,1024]{2,1,0:T(8,128)S(1)} %collective-permute-done.17.refs_2_), channel_id=1, source_target_pairs={{0,16},{16,0},{1,17},{17,1},{2,18},{18,2},{3,19},{19,3},{4,20},{20... | collective-permute-start | bytes 393224 | tf_op jit(solution)/shard_map/ppermute | solution.py:338
  72.0 8.7 %collective-permute-start.26 = (f32[4,8,1024]{2,1,0:T(8,128)S(1)}, f32[4,8,1024]{2,1,0:T(8,128)S(1)}, u32[]{:S(2)}, u32[]{:S(2)}) collective-permute-start(f32[4,8,1024]{2,1,0:T(8,128)S(1)} %collective-permute-done.16.refs_1_), channel_id=1, source_target_pairs={{0,16},{16,0},{1,17},{17,1},{2,18},{18,2},{3,19},{19,3},{4,20},{20... | collective-permute-start | bytes 393224 | tf_op jit(solution)/shard_map/ppermute | solution.py:338

commit v2 on v1

--- a/solution.py
+++ b/solution.py
@@ -167,13 +167,32 @@
             ref[:, width + LANES : width + 2 * LANES] = ref[:, LANES : 2 * LANES]
 
     window = TILE + 2 * LANES
-    shape = (window, TILE)
-    place = (
-        lax.broadcasted_iota(jnp.int32, shape, 0)
-        - lax.broadcasted_iota(jnp.int32, shape, 1)
-        + (radius - LANES)
-    )
+    tall = LANES + 2 * PACKED
+    place = iota((tall, LANES), 0) - iota((tall, LANES), 1) + (radius - PACKED)
     bands = (toeplitz(x_taps, place), toeplitz(x_taps[::-1], place))
+
+    def cut_band(band, x):
+        columns = []
+        for column in range(0, TILE, LANES):
+            above = column + LANES - PACKED
+            source = (iota((tall, 1), 0) + (x + column - PACKED + width)) % width
+            target = iota((1, LANES), 1) + (x + column)
+            apart = x_position(source, width, shift, flip_x) - x_position(target, width, shift, flip_x)
+            parts = split(jnp.where(jnp.abs(apart) <= radius, band, 0.0))
+            columns.append(
+                [
+                    jnp.concatenate(
+                        [
+                            jnp.zeros((above, LANES), part.dtype),
+                            part,
+                            jnp.zeros((window - above - tall, LANES), part.dtype),
+                        ]
+                    )
+                    for part in parts
+                ]
+            )
+        return [jnp.concatenate(parts, axis=1) for parts in zip(*columns)]
+
     lines = depth * rows
     lines_at = min(TILE, lines)
     top = chunk * rows
@@ -181,10 +200,7 @@
     def filter_x(band, store):
         wrap()
         for x in range(0, width, TILE):
-            source = (lax.broadcasted_iota(jnp.int32, (window, 1), 0) + (x - LANES + width)) % width
-            target = lax.broadcasted_iota(jnp.int32, (1, TILE), 1) + x
-            apart = x_position(source, width, shift, flip_x) - x_position(target, width, shift, flip_x)
-            cut = split(jnp.where(jnp.abs(apart) <= radius, band, 0.0))
+            cut = cut_band(band, x)
             for line in range(0, lines, lines_at):
                 at = slice(line, line + lines_at)
                 cells = (high_ref[at, x : x + window], low_ref[at, x : x + window])

time: 83.4 us -> 83.3 us (level)
  waiting for transfers between devices: 23 us -> 25.1 us
  local copies, waits for them, and re-layouts: 6.31 us -> 5.02 us
    ppermute x24, waiting for transfers between devices: 15.1 us -> 17.5 us  [send(): lax.ppermute(part, 'slab', [(i, i ^ k * unit) for i in range(slabs)])]
    rev x2 -> x0, local copies, waits for them, and re-layouts: 1.08 us -> none  [the longest x1 0.98 us: body(): jnp.flip(arr, 2)]
    ppermute x1, starting transfers between devices: 1.1 us -> 2.06 us  [body(): other_psf = lax.ppermute(late_psf, 'view', swap)]
    ppermute x4, starting transfers between devices: 4.52 us -> 3.65 us  [body(): other += [lax.ppermute(part, 'view', swap) for part in returned]]
  transfers between devices with their start and end apart: 31 -> 31, of which waited for: 12 -> 14; matrix products, arithmetic and copies ran while one was open for 6% -> 5% of each run, Pallas kernels for 12% -> 11%
where the time goes in v2:
time: 83.3 us; the launch traced here: 83 us
  starting transfers between devices  36.9 us (44%)
  waiting for transfers between devices  25.1 us (30%)
  Pallas kernels  12.8 us (15%)
  local copies, waits for them, and re-layouts  5.02 us (6%)
  between operations  2.36 us (3%)
    ppermute x24, starting transfers between devices, send(): lax.ppermute(part, 'slab', [(i, i ^ k * unit) for i in range(slabs)])  29.3 us
    ppermute x24, waiting for transfers between devices, send(): lax.ppermute(part, 'slab', [(i, i ^ k * unit) for i in range(slabs)])  17.5 us
    ppermute x4, waiting for transfers between devices, body(): other += [lax.ppermute(part, 'view', swap) for part in returned]  6.81 us
    pallas_call x2, Pallas kernels, body(): pl.pallas_call(functools.partial(ratio_kernel, chunk), out_shape=shapes(B...  6.51 us
    pallas_call x2, Pallas kernels, multiply(): pl.pallas_call(product_kernel, out_shape=jax.ShapeDtypeStruct(estimate.sh...  3.98 us
    ppermute x4, starting transfers between devices, body(): other += [lax.ppermute(part, 'view', swap) for part in returned]  3.65 us
    slice x16, local copies, waits for them, and re-layouts, exchange(): part[at]  2.41 us
    pallas_call x2, Pallas kernels, body(): pl.pallas_call(functools.partial(blur_y_kernel, chunk), out_shape=shapes(...  2.29 us
  transfers between devices with their start and end apart: 31, of which 14 were waited for; matrix products, arithmetic and copies ran while one was open for 5% of the time, Pallas kernels for 11%

profile of v2, /device:TPU:0, one launch (start us, length us, event | category | flops | bytes accessed | tf_op | source)
XLA Modules:
  0.0 83.0 jit_solution(8613203415723137681)
XLA Ops:
  0.0 0.7 copy.9.psf_ref
  0.7 1.2 %copy-done = f32[1,256,1024]{2,1,0:T(8,128)S(1)} copy-done((f32[1,256,1024]{2,1,0:T(8,128)S(1)}, f32[1,256,1024]{2,1,0:T(8,128)}, u32[]{:S(2)}) %copy-start) | copy-done | bytes 1048600
  1.9 1.1 %blur_y.2 = (f32[4,8,1024]{2,1,0:T(8,128)S(1)}, f32[4,8,1024]{2,1,0:T(8,128)S(1)}, f32[4,8,1024]{2,1,0:T(8,128)S(1)}, f32[4,8,1024]{2,1,0:T(8,128)S(1)}) custom-call(f32[1,3,17]{2,1,0:T(4,128)S(1)} %copy.9.psf_ref, f32[1,256,1024]{2,1,0:T(8,128)S(1)} %copy-done), custom_call_target="tpu_custom_call" | custom-call | bytes 6291456 | tf_op jit(solution)/shard_map/blur_y/pallas_call | solution.py:312
  3.1 3.1 %collective-permute-start = (f32[4,8,1024]{2,1,0:T(8,128)S(1)}, f32[4,8,1024]{2,1,0:T(8,128)}, u32[]{:S(2)}, u32[]{:S(2)}) collective-permute-start(f32[4,8,1024]{2,1,0:T(8,128)S(1)} %get-tuple-element.34), channel_id=1, source_target_pairs={{0,4},{1,5},{2,6},{3,7},{4,0},{5,1},{6,2},{7,3},{8,12},{9,13},{10,... | collective-permute-start | bytes 393224 | tf_op jit(solution)/shard_map/ppermute | solution.py:300
  6.2 2.6 %collective-permute-start.1 = (f32[4,8,1024]{2,1,0:T(8,128)S(1)}, f32[4,8,1024]{2,1,0:T(8,128)}, u32[]{:S(2)}, u32[]{:S(2)}) collective-permute-start(f32[4,8,1024]{2,1,0:T(8,128)S(1)} %get-tuple-element.35), channel_id=1, source_target_pairs={{0,8},{1,9},{2,10},{3,11},{4,12},{5,13},{6,14},{7,15},{8,0},{9,1},... | collective-permute-start | bytes 393224 | tf_op jit(solution)/shard_map/ppermute | solution.py:300
  8.7 1.1 %blur_y.3 = (f32[4,8,1024]{2,1,0:T(8,128)S(1)}, f32[4,8,1024]{2,1,0:T(8,128)S(1)}, f32[4,8,1024]{2,1,0:T(8,128)S(1)}, f32[4,8,1024]{2,1,0:T(8,128)S(1)}) custom-call(f32[1,3,17]{2,1,0:T(4,128)S(1)} %copy.9.psf_ref, f32[1,256,1024]{2,1,0:T(8,128)S(1)} %copy-done, f32[4,8,1024]{2,1,0:T(8,128)S(1)} %get-tuple-element.33.refs_0_), custom_call_target="tpu_custom_call" | custom-call | bytes 6291456 | tf_op jit(solution)/shard_map/blur_y/pallas_call | solution.py:312
  9.9 0.1 collective-permute-start.6
  10.0 1.8 %collective-permute-start.7 = (f32[4,8,1024]{2,1,0:T(8,128)S(1)}, f32[4,8,1024]{2,1,0:T(8,128)S(1)}, u32[]{:S(2)}, u32[]{:S(2)}) collective-permute-start(f32[4,8,1024]{2,1,0:T(8,128)S(1)} %get-tuple-element.41), channel_id=1, source_target_pairs={{0,2},{1,3},{2,0},{3,1},{4,6},{5,7},{6,4},{7,5},{8,10},{9,11},{10,... | collective-permute-start | bytes 393224 | tf_op jit(solution)/shard_map/ppermute | solution.py:300
  12.4 0.6 fusion.14
  13.1 0.6 fusion.18
  14.9 0.6 fusion
  15.6 0.0 copy-start.5
  15.7 0.0 collective-permute-done
  15.7 0.2 collective-permute-start.8
  15.8 0.8 fusion.15
  16.6 2.5 %collective-permute-done.1 = f32[4,8,1024]{2,1,0:T(8,128)} collective-permute-done((f32[4,8,1024]{2,1,0:T(8,128)S(1)}, f32[4,8,1024]{2,1,0:T(8,128)}, u32[]{:S(2)}, u32[]{:S(2)}) %collective-permute-start.1) | collective-permute-done | bytes 131104 | tf_op jit(solution)/shard_map/ppermute | solution.py:300
  19.2 0.8 fusion.16
  20.0 0.0 collective-permute-done.2
  20.1 0.1 collective-permute-start.3
  20.2 1.6 %collective-permute-start.4 = (f32[4,8,1024]{2,1,0:T(8,128)S(1)}, f32[4,8,1024]{2,1,0:T(8,128)S(1)}, u32[]{:S(2)}, u32[]{:S(2)}) collective-permute-start(f32[4,8,1024]{2,1,0:T(8,128)S(1)} %pad_maximum_fusion.3), channel_id=1, source_target_pairs={{0,2},{1,3},{2,0},{3,1},{4,6},{5,7},{6,4},{7,5},{8,10},{9,11},{10,... | collective-permute-start | bytes 393224 | tf_op jit(solution)/shard_map/ppermute | solution.py:300
  21.8 0.0 collective-permute-done.6
  21.8 0.4 collective-permute-start.5
  22.3 2.1 %collective-permute-start.10 = (f32[4,8,1024]{2,1,0:T(8,128)S(1)}, f32[4,8,1024]{2,1,0:T(8,128)S(1)}, u32[]{:S(2)}, u32[]{:S(2)}) collective-permute-start(f32[4,8,1024]{2,1,0:T(8,128)S(1)} %pad_maximum_fusion.7), channel_id=1, source_target_pairs={{0,8},{1,9},{2,10},{3,11},{4,12},{5,13},{6,14},{7,15},{8,0},{9,1},... | collective-permute-start | bytes 393224 | tf_op jit(solution)/shard_map/ppermute | solution.py:300
  24.4 1.4 %collective-permute-start.11 = (f32[4,8,1024]{2,1,0:T(8,128)S(1)}, f32[4,8,1024]{2,1,0:T(8,128)S(1)}, u32[]{:S(2)}, u32[]{:S(2)}) collective-permute-start(f32[4,8,1024]{2,1,0:T(8,128)S(1)} %pad_maximum_fusion.8), channel_id=1, source_target_pairs={{0,12},{1,13},{2,14},{3,15},{4,8},{5,9},{6,10},{7,11},{8,4},{9,5},... | collective-permute-start | bytes 393224 | tf_op jit(solution)/shard_map/ppermute | solution.py:300
  25.9 0.0 collective-permute-done.3.refs_1_
  25.9 0.2 collective-permute-start.9
  26.0 0.5 collective-permute-done.4.refs_2_
  26.5 2.0 %collective-permute-done.5.refs_3_ = f32[4,8,1024]{2,1,0:T(8,128)S(1)} collective-permute-done((f32[4,8,1024]{2,1,0:T(8,128)S(1)}, f32[4,8,1024]{2,1,0:T(8,128)S(1)}, u32[]{:S(2)}, u32[]{:S(2)}) %collective-permute-start.5) | collective-permute-done | bytes 131104 | tf_op jit(solution)/shard_map/ppermute | solution.py:300
  28.5 3.2 %ratio.2 = (f32[4,8,1024]{2,1,0:T(8,128)S(1)}, f32[4,8,1024]{2,1,0:T(8,128)S(1)}, f32[4,8,1024]{2,1,0:T(8,128)S(1)}, f32[4,8,1024]{2,1,0:T(8,128)S(1)}) custom-call(s32[1]{0:T(128)S(6)} %copy.18.offset_ref, s32[1,2]{1,0:T(1,128)S(1)} %copy-done.2, f32[1,3,17]{2,1,0:T(4,128)S(1)} %copy.9.psf_ref, f32[16,16,1024]{2,1,0:T(8,128)S(1)} %get-tuple-element.121.meas_ref, ...), custom_call_target="tpu_custom_call" | custom-call | bytes 12582912 | tf_op jit(solution)/shard_map/ratio/pallas_call | solution.py:329
  31.8 1.1 %collective-permute-start.19 = (f32[4,8,1024]{2,1,0:T(8,128)S(1)}, f32[4,8,1024]{2,1,0:T(8,128)S(1)}, u32[]{:S(2)}, u32[]{:S(2)}) collective-permute-start(f32[4,8,1024]{2,1,0:T(8,128)S(1)} %get-tuple-element.48), channel_id=1, source_target_pairs={{0,4},{1,5},{2,6},{3,7},{4,0},{5,1},{6,2},{7,3},{8,12},{9,13},{10,... | collective-permute-start | bytes 393224 | tf_op jit(solution)/shard_map/ppermute | solution.py:300
  32.9 1.8 %collective-permute-start.20 = (f32[4,8,1024]{2,1,0:T(8,128)S(1)}, f32[4,8,1024]{2,1,0:T(8,128)S(1)}, u32[]{:S(2)}, u32[]{:S(2)}) collective-permute-start(f32[4,8,1024]{2,1,0:T(8,128)S(1)} %get-tuple-element.49), channel_id=1, source_target_pairs={{0,8},{1,9},{2,10},{3,11},{4,12},{5,13},{6,14},{7,15},{8,0},{9,1},... | collective-permute-start | bytes 393224 | tf_op jit(solution)/shard_map/ppermute | solution.py:300
  34.7 0.4 collective-permute-done.10.refs_2_
  35.1 2.5 %collective-permute-start.21 = (f32[4,8,1024]{2,1,0:T(8,128)S(1)}, f32[4,8,1024]{2,1,0:T(8,128)S(1)}, u32[]{:S(2)}, u32[]{:S(2)}) collective-permute-start(f32[4,8,1024]{2,1,0:T(8,128)S(1)} %get-tuple-element.50), channel_id=1, source_target_pairs={{0,12},{1,13},{2,14},{3,15},{4,8},{5,9},{6,10},{7,11},{8,4},{9,5},... | collective-permute-start | bytes 393224 | tf_op jit(solution)/shard_map/ppermute | solution.py:300
  37.6 3.3 %ratio.3 = (f32[4,8,1024]{2,1,0:T(8,128)S(1)}, f32[4,8,1024]{2,1,0:T(8,128)S(1)}, f32[4,8,1024]{2,1,0:T(8,128)S(1)}, f32[4,8,1024]{2,1,0:T(8,128)S(1)}) custom-call(s32[1]{0:T(128)S(6)} %copy.18.offset_ref, s32[1,2]{1,0:T(1,128)S(1)} %copy-done.2, f32[1,3,17]{2,1,0:T(4,128)S(1)} %copy.9.psf_ref, f32[16,16,1024]{2,1,0:T(8,128)S(1)} %get-tuple-element.121.meas_ref, ...), custom_call_target="tpu_custom_call" | custom-call | bytes 12582912 | tf_op jit(solution)/shard_map/ratio/pallas_call | solution.py:329
  40.9 0.1 collective-permute-start.12
  41.0 1.5 %collective-permute-start.13 = (f32[4,8,1024]{2,1,0:T(8,128)S(1)}, f32[4,8,1024]{2,1,0:T(8,128)S(1)}, u32[]{:S(2)}, u32[]{:S(2)}) collective-permute-start(f32[4,8,1024]{2,1,0:T(8,128)S(1)} %get-tuple-element.45), channel_id=1, source_target_pairs={{0,2},{1,3},{2,0},{3,1},{4,6},{5,7},{6,4},{7,5},{8,10},{9,11},{10,... | collective-permute-start | bytes 393224 | tf_op jit(solution)/shard_map/ppermute | solution.py:300
  42.4 0.5 collective-permute-start.14
  42.9 3.4 %collective-permute-done.20 = f32[4,8,1024]{2,1,0:T(8,128)S(1)} collective-permute-done((f32[4,8,1024]{2,1,0:T(8,128)S(1)}, f32[4,8,1024]{2,1,0:T(8,128)S(1)}, u32[]{:S(2)}, u32[]{:S(2)}) %collective-permute-start.20) | collective-permute-done | bytes 131104 | tf_op jit(solution)/shard_map/ppermute | solution.py:300
  46.4 0.2 collective-permute-start.24
  46.7 1.4 %collective-permute-start.23 = (f32[4,8,1024]{2,1,0:T(8,128)S(1)}, f32[4,8,1024]{2,1,0:T(8,128)S(1)}, u32[]{:S(2)}, u32[]{:S(2)}) collective-permute-start(f32[4,8,1024]{2,1,0:T(8,128)S(1)} %pad_maximum_fusion.15), channel_id=1, source_target_pairs={{0,2},{1,3},{2,0},{3,1},{4,6},{5,7},{6,4},{7,5},{8,10},{9,11},{10,... | collective-permute-start | bytes 393224 | tf_op jit(solution)/shard_map/ppermute | solution.py:300
  48.1 0.4 collective-permute-start.22
  48.6 0.0 copy-start.8
  48.6 0.6 collective-permute-done.14
  49.2 0.0 copy-start.1
  49.3 2.2 %collective-permute-start.18 = (f32[4,8,1024]{2,1,0:T(8,128)S(1)}, f32[4,8,1024]{2,1,0:T(8,128)S(1)}, u32[]{:S(2)}, u32[]{:S(2)}) collective-permute-start(f32[4,8,1024]{2,1,0:T(8,128)S(1)} %pad_maximum_fusion.12), channel_id=1, source_target_pairs={{0,12},{1,13},{2,14},{3,15},{4,8},{5,9},{6,10},{7,11},{8,4},{9,5},... | collective-permute-start | bytes 393224 | tf_op jit(solution)/shard_map/ppermute | solution.py:300
  51.5 0.9 %collective-permute-done.24.refs_7_ = f32[4,8,1024]{2,1,0:T(8,128)S(1)} collective-permute-done((f32[4,8,1024]{2,1,0:T(8,128)S(1)}, f32[4,8,1024]{2,1,0:T(8,128)S(1)}, u32[]{:S(2)}, u32[]{:S(2)}) %collective-permute-start.24) | collective-permute-done | bytes 131104 | tf_op jit(solution)/shard_map/ppermute | solution.py:300
  52.4 2.9 %collective-permute-done.23.refs_6_ = f32[4,8,1024]{2,1,0:T(8,128)S(1)} collective-permute-done((f32[4,8,1024]{2,1,0:T(8,128)S(1)}, f32[4,8,1024]{2,1,0:T(8,128)S(1)}, u32[]{:S(2)}, u32[]{:S(2)}) %collective-permute-start.23) | collective-permute-done | bytes 131104 | tf_op jit(solution)/shard_map/ppermute | solution.py:300
  55.3 1.6 %collective-permute-start.30 = (f32[12,8,1024]{2,1,0:T(8,128)S(1)}, f32[12,8,1024]{2,1,0:T(8,128)S(1)}, u32[]{:S(2)}, u32[]{:S(2)}) collective-permute-start(f32[12,8,1024]{2,1,0:T(8,128)S(1)} %pad_maximum_fusion), channel_id=1, source_target_pairs={{0,16},{16,0},{1,17},{17,1},{2,18},{18,2},{3,19},{19,3},{4,20},{20... | collective-permute-start | bytes 1179656 | tf_op jit(solution)/shard_map/ppermute | solution.py:350
  56.9 4.2 %collective-permute-start.17 = (f32[4,8,1024]{2,1,0:T(8,128)S(1)}, f32[4,8,1024]{2,1,0:T(8,128)S(1)}, u32[]{:S(2)}, u32[]{:S(2)}) collective-permute-start(f32[4,8,1024]{2,1,0:T(8,128)S(1)} %pad_maximum_fusion.11), channel_id=1, source_target_pairs={{0,8},{1,9},{2,10},{3,11},{4,12},{5,13},{6,14},{7,15},{8,0},{9,1},... | collective-permute-start | bytes 393224 | tf_op jit(solution)/shard_map/ppermute | solution.py:300
  61.1 0.1 collective-permute-start.16
  61.2 0.1 collective-permute-start.25
  61.3 2.1 %collective-permute-start.15 = (f32[1,3,17]{2,1,0:T(4,128)S(1)}, f32[1,3,17]{2,1,0:T(4,128)S(1)}, u32[]{:S(2)}, u32[]{:S(2)}) collective-permute-start(f32[1,3,17]{2,1,0:T(4,128)S(1)} %copy.10), channel_id=1, source_target_pairs={{0,16},{16,0},{1,17},{17,1},{2,18},{18,2},{3,19},{19,3},{4,20},{20... | collective-permute-start | bytes 620 | tf_op jit(solution)/shard_map/ppermute | solution.py:356
  63.4 3.9 %collective-permute-done.17.refs_2_ = f32[4,8,1024]{2,1,0:T(8,128)S(1)} collective-permute-done((f32[4,8,1024]{2,1,0:T(8,128)S(1)}, f32[4,8,1024]{2,1,0:T(8,128)S(1)}, u32[]{:S(2)}, u32[]{:S(2)}) %collective-permute-start.17) | collective-permute-done | bytes 131104 | tf_op jit(solution)/shard_map/ppermute | solution.py:300
  67.3 0.3 collective-permute-start.29
  67.6 0.3 collective-permute-done.16.refs_1_
  67.8 1.5 %collective-permute-start.28 = (f32[4,8,1024]{2,1,0:T(8,128)S(1)}, f32[4,8,1024]{2,1,0:T(8,128)S(1)}, u32[]{:S(2)}, u32[]{:S(2)}) collective-permute-start(f32[4,8,1024]{2,1,0:T(8,128)S(1)} %collective-permute-done.18.refs_3_), channel_id=1, source_target_pairs={{0,16},{16,0},{1,17},{17,1},{2,18},{18,2},{3,19},{19,3},{4,20},{20... | collective-permute-start | bytes 393224 | tf_op jit(solution)/shard_map/ppermute | solution.py:354
  69.3 1.5 %product.2.factor_ref = f32[1,256,1024]{2,1,0:T(8,128)S(1)} custom-call(f32[1,3,17]{2,1,0:T(4,128)S(1)} %copy.9.psf_ref, f32[1,256,1024]{2,1,0:T(8,128)S(1)} %copy-done.1, f32[4,8,1024]{2,1,0:T(8,128)S(1)} %pad_maximum_fusion.9.refs_0_, f32[4,8,1024]{2,1,0:T(8,128)S(1)} %collective-permute-done.16.refs_1_, ...), custom_call_target="tpu_custom_call" | custom-call | bytes 6291456 | tf_op jit(solution)/shard_map/product/pallas_call | solution.py:359
  70.8 0.9 %collective-permute-start.27 = (f32[4,8,1024]{2,1,0:T(8,128)S(1)}, f32[4,8,1024]{2,1,0:T(8,128)S(1)}, u32[]{:S(2)}, u32[]{:S(2)}) collective-permute-start(f32[4,8,1024]{2,1,0:T(8,128)S(1)} %collective-permute-done.17.refs_2_), channel_id=1, source_target_pairs={{0,16},{16,0},{1,17},{17,1},{2,18},{18,2},{3,19},{19,3},{4,20},{20... | collective-permute-start | bytes 393224 | tf_op jit(solution)/shard_map/ppermute | solution.py:354
  71.7 1.2 %collective-permute-start.26 = (f32[4,8,1024]{2,1,0:T(8,128)S(1)}, f32[4,8,1024]{2,1,0:T(8,128)S(1)}, u32[]{:S(2)}, u32[]{:S(2)}) collective-permute-start(f32[4,8,1024]{2,1,0:T(8,128)S(1)} %collective-permute-done.16.refs_1_), channel_id=1, source_target_pairs={{0,16},{16,0},{1,17},{17,1},{2,18},{18,2},{3,19},{19,3},{4,20},{20... | collective-permute-start | bytes 393224 | tf_op jit(solution)/shard_map/ppermute | solution.py:354
  72.9 0.8 collective-permute-done.29.refs_4_
  73.7 2.8 %collective-permute-done.28.refs_3_ = f32[4,8,1024]{2,1,0:T(8,128)S(1)} collective-permute-done((f32[4,8,1024]{2,1,0:T(8,128)S(1)}, f32[4,8,1024]{2,1,0:T(8,128)S(1)}, u32[]{:S(2)}, u32[]{:S(2)}) %collective-permute-start.28) | collective-permute-done | bytes 131104 | tf_op jit(solution)/shard_map/ppermute | solution.py:354
  76.5 2.6 %collective-permute-done.27.refs_2_ = f32[4,8,1024]{2,1,0:T(8,128)S(1)} collective-permute-done((f32[4,8,1024]{2,1,0:T(8,128)S(1)}, f32[4,8,1024]{2,1,0:T(8,128)S(1)}, u32[]{:S(2)}, u32[]{:S(2)}) %collective-permute-start.27) | collective-permute-done | bytes 131104 | tf_op jit(solution)/shard_map/ppermute | solution.py:354
  79.1 1.4 %collective-permute-done.26.refs_1_ = f32[4,8,1024]{2,1,0:T(8,128)S(1)} collective-permute-done((f32[4,8,1024]{2,1,0:T(8,128)S(1)}, f32[4,8,1024]{2,1,0:T(8,128)S(1)}, u32[]{:S(2)}, u32[]{:S(2)}) %collective-permute-start.26) | collective-permute-done | bytes 131104 | tf_op jit(solution)/shard_map/ppermute | solution.py:354
  80.5 2.5 %product.3 = f32[1,256,1024]{2,1,0:T(8,128)} custom-call(f32[1,3,17]{2,1,0:T(4,128)S(1)} %collective-permute-done.15.psf_ref, f32[1,256,1024]{2,1,0:T(8,128)S(1)} %product.2.factor_ref, f32[4,8,1024]{2,1,0:T(8,128)S(1)} %collective-permute-done.25.refs_0_, f32[4,8,1024]{2,1,0:T(8,128)S(1)} %collective-permute-done.26.refs_1_, ...), custom_call_target="tpu_custom_call" | custom-call | bytes 6291456 | tf_op jit(solution)/shard_map/product/pallas_call | solution.py:359
  (62 shorter events, 0.5 us)
Async XLA Ops:
  0.7 1.2 %copy-start = (f32[1,256,1024]{2,1,0:T(8,128)S(1)}, f32[1,256,1024]{2,1,0:T(8,128)}, u32[]{:S(2)}) copy-start(f32[1,256,1024]{2,1,0:T(8,128)} %factor_ref.1) | copy-start | bytes 3145732
  1.9 11.1 %copy-start.2 = (s32[1,2]{1,0:T(1,128)S(1)}, s32[1,2]{1,0:T(1,128)}, u32[]{:S(2)}) copy-start(s32[1,2]{1,0:T(1,128)} %mirror_ref.3) | copy-start | bytes 28
  1.9 13.0 %copy-start.3 = (f32[1,16,16,1024]{3,2,1,0:T(8,128)S(1)}, f32[1,16,16,1024]{3,2,1,0:T(8,128)}, u32[]{:S(2)}) copy-start(f32[1,16,16,1024]{3,2,1,0:T(8,128)} %param.10) | copy-start | bytes 3145732
  3.1 12.6 %collective-permute-start = (f32[4,8,1024]{2,1,0:T(8,128)S(1)}, f32[4,8,1024]{2,1,0:T(8,128)}, u32[]{:S(2)}, u32[]{:S(2)}) collective-permute-start(f32[4,8,1024]{2,1,0:T(8,128)S(1)} %get-tuple-element.34), channel_id=1, source_target_pairs={{0,4},{1,5},{2,6},{3,7},{4,0},{5,1},{6,2},{7,3},{8,12},{9,13},{10,... | collective-permute-start | bytes 393224 | tf_op jit(solution)/shard_map/ppermute | solution.py:300
  6.2 13.0 %collective-permute-start.1 = (f32[4,8,1024]{2,1,0:T(8,128)S(1)}, f32[4,8,1024]{2,1,0:T(8,128)}, u32[]{:S(2)}, u32[]{:S(2)}) collective-permute-start(f32[4,8,1024]{2,1,0:T(8,128)S(1)} %get-tuple-element.35), channel_id=1, source_target_pairs={{0,8},{1,9},{2,10},{3,11},{4,12},{5,13},{6,14},{7,15},{8,0},{9,1},... | collective-permute-start | bytes 393224 | tf_op jit(solution)/shard_map/ppermute | solution.py:300
  8.7 11.3 %collective-permute-start.2 = (f32[4,8,1024]{2,1,0:T(8,128)S(1)}, f32[4,8,1024]{2,1,0:T(8,128)S(1)}, u32[]{:S(2)}, u32[]{:S(2)}) collective-permute-start(f32[4,8,1024]{2,1,0:T(8,128)S(1)} %get-tuple-element.36), channel_id=1, source_target_pairs={{0,12},{1,13},{2,14},{3,15},{4,8},{5,9},{6,10},{7,11},{8,4},{9,5},... | collective-permute-start | bytes 393224 | tf_op jit(solution)/shard_map/ppermute | solution.py:300
  9.9 11.9 %collective-permute-start.6 = (f32[4,8,1024]{2,1,0:T(8,128)S(1)}, f32[4,8,1024]{2,1,0:T(8,128)S(1)}, u32[]{:S(2)}, u32[]{:S(2)}) collective-permute-start(f32[4,8,1024]{2,1,0:T(8,128)S(1)} %get-tuple-element.40), channel_id=1, source_target_pairs={{0,1},{1,0},{2,3},{3,2},{4,5},{5,4},{6,7},{7,6},{8,9},{9,8},{10,11... | collective-permute-start | bytes 393224 | tf_op jit(solution)/shard_map/ppermute | solution.py:300
  10.0 12.2 %collective-permute-start.7 = (f32[4,8,1024]{2,1,0:T(8,128)S(1)}, f32[4,8,1024]{2,1,0:T(8,128)S(1)}, u32[]{:S(2)}, u32[]{:S(2)}) collective-permute-start(f32[4,8,1024]{2,1,0:T(8,128)S(1)} %get-tuple-element.41), channel_id=1, source_target_pairs={{0,2},{1,3},{2,0},{3,1},{4,6},{5,7},{6,4},{7,5},{8,10},{9,11},{10,... | collective-permute-start | bytes 393224 | tf_op jit(solution)/shard_map/ppermute | solution.py:300
  15.6 4.4 %copy-start.7 = (f32[1,8,1024]{2,1,0:T(8,128)S(1)}, f32[1,8,1024]{2,1,0:T(8,128)}, u32[]{:S(2)}) copy-start(f32[1,8,1024]{2,1,0:T(8,128)} %get-tuple-element.104) | copy-start | bytes 98308
  15.6 4.5 %copy-start.6 = (f32[1,8,1024]{2,1,0:T(8,128)S(1)}, f32[1,8,1024]{2,1,0:T(8,128)}, u32[]{:S(2)}) copy-start(f32[1,8,1024]{2,1,0:T(8,128)} %get-tuple-element.103) | copy-start | bytes 98308
  15.6 6.1 %copy-start.5 = (f32[1,8,1024]{2,1,0:T(8,128)S(1)}, f32[1,8,1024]{2,1,0:T(8,128)}, u32[]{:S(2)}) copy-start(f32[1,8,1024]{2,1,0:T(8,128)} %get-tuple-element.102) | copy-start | bytes 98308
  15.7 6.6 %collective-permute-start.8 = (f32[4,8,1024]{2,1,0:T(8,128)S(1)}, f32[4,8,1024]{2,1,0:T(8,128)S(1)}, u32[]{:S(2)}, u32[]{:S(2)}) collective-permute-start(f32[4,8,1024]{2,1,0:T(8,128)S(1)} %get-tuple-element.42), channel_id=1, source_target_pairs={{0,3},{1,2},{2,1},{3,0},{4,7},{5,6},{6,5},{7,4},{8,11},{9,10},{10,... | collective-permute-start | bytes 393224 | tf_op jit(solution)/shard_map/ppermute | solution.py:300
  20.0 5.8 %copy-start.4 = (f32[1,8,1024]{2,1,0:T(8,128)S(1)}, f32[1,8,1024]{2,1,0:T(8,128)}, u32[]{:S(2)}) copy-start(f32[1,8,1024]{2,1,0:T(8,128)} %get-tuple-element.105) | copy-start | bytes 98308
  20.1 5.8 %collective-permute-start.3 = (f32[4,8,1024]{2,1,0:T(8,128)S(1)}, f32[4,8,1024]{2,1,0:T(8,128)S(1)}, u32[]{:S(2)}, u32[]{:S(2)}) collective-permute-start(f32[4,8,1024]{2,1,0:T(8,128)S(1)} %pad_maximum_fusion.2), channel_id=1, source_target_pairs={{0,1},{1,0},{2,3},{3,2},{4,5},{5,4},{6,7},{7,6},{8,9},{9,8},{10,11... | collective-permute-start | bytes 393224 | tf_op jit(solution)/shard_map/ppermute | solution.py:300
  20.2 6.4 %collective-permute-start.4 = (f32[4,8,1024]{2,1,0:T(8,128)S(1)}, f32[4,8,1024]{2,1,0:T(8,128)S(1)}, u32[]{:S(2)}, u32[]{:S(2)}) collective-permute-start(f32[4,8,1024]{2,1,0:T(8,128)S(1)} %pad_maximum_fusion.3), channel_id=1, source_target_pairs={{0,2},{1,3},{2,0},{3,1},{4,6},{5,7},{6,4},{7,5},{8,10},{9,11},{10,... | collective-permute-start | bytes 393224 | tf_op jit(solution)/shard_map/ppermute | solution.py:300
  21.8 6.8 %collective-permute-start.5 = (f32[4,8,1024]{2,1,0:T(8,128)S(1)}, f32[4,8,1024]{2,1,0:T(8,128)S(1)}, u32[]{:S(2)}, u32[]{:S(2)}) collective-permute-start(f32[4,8,1024]{2,1,0:T(8,128)S(1)} %pad_maximum_fusion.4), channel_id=1, source_target_pairs={{0,3},{1,2},{2,1},{3,0},{4,7},{5,6},{6,5},{7,4},{8,11},{9,10},{10,... | collective-permute-start | bytes 393224 | tf_op jit(solution)/shard_map/ppermute | solution.py:300
  22.3 12.8 %collective-permute-start.10 = (f32[4,8,1024]{2,1,0:T(8,128)S(1)}, f32[4,8,1024]{2,1,0:T(8,128)S(1)}, u32[]{:S(2)}, u32[]{:S(2)}) collective-permute-start(f32[4,8,1024]{2,1,0:T(8,128)S(1)} %pad_maximum_fusion.7), channel_id=1, source_target_pairs={{0,8},{1,9},{2,10},{3,11},{4,12},{5,13},{6,14},{7,15},{8,0},{9,1},... | collective-permute-start | bytes 393224 | tf_op jit(solution)/shard_map/ppermute | solution.py:300
  24.4 13.2 %collective-permute-start.11 = (f32[4,8,1024]{2,1,0:T(8,128)S(1)}, f32[4,8,1024]{2,1,0:T(8,128)S(1)}, u32[]{:S(2)}, u32[]{:S(2)}) collective-permute-start(f32[4,8,1024]{2,1,0:T(8,128)S(1)} %pad_maximum_fusion.8), channel_id=1, source_target_pairs={{0,12},{1,13},{2,14},{3,15},{4,8},{5,9},{6,10},{7,11},{8,4},{9,5},... | collective-permute-start | bytes 393224 | tf_op jit(solution)/shard_map/ppermute | solution.py:300
  25.9 11.8 %collective-permute-start.9 = (f32[4,8,1024]{2,1,0:T(8,128)S(1)}, f32[4,8,1024]{2,1,0:T(8,128)S(1)}, u32[]{:S(2)}, u32[]{:S(2)}) collective-permute-start(f32[4,8,1024]{2,1,0:T(8,128)S(1)} %pad_maximum_fusion.6), channel_id=1, source_target_pairs={{0,4},{1,5},{2,6},{3,7},{4,0},{5,1},{6,2},{7,3},{8,12},{9,13},{10,... | collective-permute-start | bytes 393224 | tf_op jit(solution)/shard_map/ppermute | solution.py:300
  31.8 10.6 %collective-permute-start.19 = (f32[4,8,1024]{2,1,0:T(8,128)S(1)}, f32[4,8,1024]{2,1,0:T(8,128)S(1)}, u32[]{:S(2)}, u32[]{:S(2)}) collective-permute-start(f32[4,8,1024]{2,1,0:T(8,128)S(1)} %get-tuple-element.48), channel_id=1, source_target_pairs={{0,4},{1,5},{2,6},{3,7},{4,0},{5,1},{6,2},{7,3},{8,12},{9,13},{10,... | collective-permute-start | bytes 393224 | tf_op jit(solution)/shard_map/ppermute | solution.py:300
  32.9 13.5 %collective-permute-start.20 = (f32[4,8,1024]{2,1,0:T(8,128)S(1)}, f32[4,8,1024]{2,1,0:T(8,128)S(1)}, u32[]{:S(2)}, u32[]{:S(2)}) collective-permute-start(f32[4,8,1024]{2,1,0:T(8,128)S(1)} %get-tuple-element.49), channel_id=1, source_target_pairs={{0,8},{1,9},{2,10},{3,11},{4,12},{5,13},{6,14},{7,15},{8,0},{9,1},... | collective-permute-start | bytes 393224 | tf_op jit(solution)/shard_map/ppermute | solution.py:300
  35.1 11.3 %collective-permute-start.21 = (f32[4,8,1024]{2,1,0:T(8,128)S(1)}, f32[4,8,1024]{2,1,0:T(8,128)S(1)}, u32[]{:S(2)}, u32[]{:S(2)}) collective-permute-start(f32[4,8,1024]{2,1,0:T(8,128)S(1)} %get-tuple-element.50), channel_id=1, source_target_pairs={{0,12},{1,13},{2,14},{3,15},{4,8},{5,9},{6,10},{7,11},{8,4},{9,5},... | collective-permute-start | bytes 393224 | tf_op jit(solution)/shard_map/ppermute | solution.py:300
  40.9 7.2 %collective-permute-start.12 = (f32[4,8,1024]{2,1,0:T(8,128)S(1)}, f32[4,8,1024]{2,1,0:T(8,128)S(1)}, u32[]{:S(2)}, u32[]{:S(2)}) collective-permute-start(f32[4,8,1024]{2,1,0:T(8,128)S(1)} %get-tuple-element.44), channel_id=1, source_target_pairs={{0,1},{1,0},{2,3},{3,2},{4,5},{5,4},{6,7},{7,6},{8,9},{9,8},{10,11... | collective-permute-start | bytes 393224 | tf_op jit(solution)/shard_map/ppermute | solution.py:300
  41.0 7.6 %collective-permute-start.13 = (f32[4,8,1024]{2,1,0:T(8,128)S(1)}, f32[4,8,1024]{2,1,0:T(8,128)S(1)}, u32[]{:S(2)}, u32[]{:S(2)}) collective-permute-start(f32[4,8,1024]{2,1,0:T(8,128)S(1)} %get-tuple-element.45), channel_id=1, source_target_pairs={{0,2},{1,3},{2,0},{3,1},{4,6},{5,7},{6,4},{7,5},{8,10},{9,11},{10,... | collective-permute-start | bytes 393224 | tf_op jit(solution)/shard_map/ppermute | solution.py:300
  42.4 6.8 %collective-permute-start.14 = (f32[4,8,1024]{2,1,0:T(8,128)S(1)}, f32[4,8,1024]{2,1,0:T(8,128)S(1)}, u32[]{:S(2)}, u32[]{:S(2)}) collective-permute-start(f32[4,8,1024]{2,1,0:T(8,128)S(1)} %get-tuple-element.46), channel_id=1, source_target_pairs={{0,3},{1,2},{2,1},{3,0},{4,7},{5,6},{6,5},{7,4},{8,11},{9,10},{10,... | collective-permute-start | bytes 393224 | tf_op jit(solution)/shard_map/ppermute | solution.py:300
  46.4 5.9 %collective-permute-start.24 = (f32[4,8,1024]{2,1,0:T(8,128)S(1)}, f32[4,8,1024]{2,1,0:T(8,128)S(1)}, u32[]{:S(2)}, u32[]{:S(2)}) collective-permute-start(f32[4,8,1024]{2,1,0:T(8,128)S(1)} %pad_maximum_fusion.16), channel_id=1, source_target_pairs={{0,3},{1,2},{2,1},{3,0},{4,7},{5,6},{6,5},{7,4},{8,11},{9,10},{10,... | collective-permute-start | bytes 393224 | tf_op jit(solution)/shard_map/ppermute | solution.py:300
  46.7 8.6 %collective-permute-start.23 = (f32[4,8,1024]{2,1,0:T(8,128)S(1)}, f32[4,8,1024]{2,1,0:T(8,128)S(1)}, u32[]{:S(2)}, u32[]{:S(2)}) collective-permute-start(f32[4,8,1024]{2,1,0:T(8,128)S(1)} %pad_maximum_fusion.15), channel_id=1, source_target_pairs={{0,2},{1,3},{2,0},{3,1},{4,6},{5,7},{6,4},{7,5},{8,10},{9,11},{10,... | collective-permute-start | bytes 393224 | tf_op jit(solution)/shard_map/ppermute | solution.py:300
  48.1 7.2 %collective-permute-start.22 = (f32[4,8,1024]{2,1,0:T(8,128)S(1)}, f32[4,8,1024]{2,1,0:T(8,128)S(1)}, u32[]{:S(2)}, u32[]{:S(2)}) collective-permute-start(f32[4,8,1024]{2,1,0:T(8,128)S(1)} %pad_maximum_fusion.14), channel_id=1, source_target_pairs={{0,1},{1,0},{2,3},{3,2},{4,5},{5,4},{6,7},{7,6},{8,9},{9,8},{10,11... | collective-permute-start | bytes 393224 | tf_op jit(solution)/shard_map/ppermute | solution.py:300
  48.6 12.7 %copy-start.8 = (f32[1,3,17]{2,0,1:T(1,128)S(1)}, f32[1,3,17]{2,0,1:T(1,128)}, u32[]{:S(2)}) copy-start(f32[1,3,17]{2,0,1:T(1,128)} %param.13) | copy-start | bytes 616
  49.2 20.0 %copy-start.1 = (f32[1,256,1024]{2,1,0:T(8,128)S(1)}, f32[1,256,1024]{2,1,0:T(8,128)}, u32[]{:S(2)}) copy-start(f32[1,256,1024]{2,1,0:T(8,128)} %factor_ref.1) | copy-start | bytes 3145732
  49.3 12.0 %collective-permute-start.18 = (f32[4,8,1024]{2,1,0:T(8,128)S(1)}, f32[4,8,1024]{2,1,0:T(8,128)S(1)}, u32[]{:S(2)}, u32[]{:S(2)}) collective-permute-start(f32[4,8,1024]{2,1,0:T(8,128)S(1)} %pad_maximum_fusion.12), channel_id=1, source_target_pairs={{0,12},{1,13},{2,14},{3,15},{4,8},{5,9},{6,10},{7,11},{8,4},{9,5},... | collective-permute-start | bytes 393224 | tf_op jit(solution)/shard_map/ppermute | solution.py:300
  55.3 16.4 %collective-permute-start.30 = (f32[12,8,1024]{2,1,0:T(8,128)S(1)}, f32[12,8,1024]{2,1,0:T(8,128)S(1)}, u32[]{:S(2)}, u32[]{:S(2)}) collective-permute-start(f32[12,8,1024]{2,1,0:T(8,128)S(1)} %pad_maximum_fusion), channel_id=1, source_target_pairs={{0,16},{16,0},{1,17},{17,1},{2,18},{18,2},{3,19},{19,3},{4,20},{20... | collective-permute-start | bytes 1179656 | tf_op jit(solution)/shard_map/ppermute | solution.py:350
  56.9 10.3 %collective-permute-start.17 = (f32[4,8,1024]{2,1,0:T(8,128)S(1)}, f32[4,8,1024]{2,1,0:T(8,128)S(1)}, u32[]{:S(2)}, u32[]{:S(2)}) collective-permute-start(f32[4,8,1024]{2,1,0:T(8,128)S(1)} %pad_maximum_fusion.11), channel_id=1, source_target_pairs={{0,8},{1,9},{2,10},{3,11},{4,12},{5,13},{6,14},{7,15},{8,0},{9,1},... | collective-permute-start | bytes 393224 | tf_op jit(solution)/shard_map/ppermute | solution.py:300
  61.1 6.7 %collective-permute-start.16 = (f32[4,8,1024]{2,1,0:T(8,128)S(1)}, f32[4,8,1024]{2,1,0:T(8,128)S(1)}, u32[]{:S(2)}, u32[]{:S(2)}) collective-permute-start(f32[4,8,1024]{2,1,0:T(8,128)S(1)} %pad_maximum_fusion.10), channel_id=1, source_target_pairs={{0,4},{1,5},{2,6},{3,7},{4,0},{5,1},{6,2},{7,3},{8,12},{9,13},{10,... | collective-permute-start | bytes 393224 | tf_op jit(solution)/shard_map/ppermute | solution.py:300
  61.2 12.5 %collective-permute-start.25 = (f32[4,8,1024]{2,1,0:T(8,128)S(1)}, f32[4,8,1024]{2,1,0:T(8,128)S(1)}, u32[]{:S(2)}, u32[]{:S(2)}) collective-permute-start(f32[4,8,1024]{2,1,0:T(8,128)S(1)} %pad_maximum_fusion.9.refs_0_), channel_id=1, source_target_pairs={{0,16},{16,0},{1,17},{17,1},{2,18},{18,2},{3,19},{19,3},{4,20},{20... | collective-permute-start | bytes 393224 | tf_op jit(solution)/shard_map/ppermute | solution.py:354
  61.3 9.5 %collective-permute-start.15 = (f32[1,3,17]{2,1,0:T(4,128)S(1)}, f32[1,3,17]{2,1,0:T(4,128)S(1)}, u32[]{:S(2)}, u32[]{:S(2)}) collective-permute-start(f32[1,3,17]{2,1,0:T(4,128)S(1)} %copy.10), channel_id=1, source_target_pairs={{0,16},{16,0},{1,17},{17,1},{2,18},{18,2},{3,19},{19,3},{4,20},{20... | collective-permute-start | bytes 620 | tf_op jit(solution)/shard_map/ppermute | solution.py:356
  67.3 6.4 %collective-permute-start.29 = (f32[4,8,1024]{2,1,0:T(8,128)S(1)}, f32[4,8,1024]{2,1,0:T(8,128)S(1)}, u32[]{:S(2)}, u32[]{:S(2)}) collective-permute-start(f32[4,8,1024]{2,1,0:T(8,128)S(1)} %pad_maximum_fusion.13.refs_4_), channel_id=1, source_target_pairs={{0,16},{16,0},{1,17},{17,1},{2,18},{18,2},{3,19},{19,3},{4,20},{20... | collective-permute-start | bytes 393224 | tf_op jit(solution)/shard_map/ppermute | solution.py:351
  67.8 8.7 %collective-permute-start.28 = (f32[4,8,1024]{2,1,0:T(8,128)S(1)}, f32[4,8,1024]{2,1,0:T(8,128)S(1)}, u32[]{:S(2)}, u32[]{:S(2)}) collective-permute-start(f32[4,8,1024]{2,1,0:T(8,128)S(1)} %collective-permute-done.18.refs_3_), channel_id=1, source_target_pairs={{0,16},{16,0},{1,17},{17,1},{2,18},{18,2},{3,19},{19,3},{4,20},{20... | collective-permute-start | bytes 393224 | tf_op jit(solution)/shard_map/ppermute | solution.py:354
  70.8 8.3 %collective-permute-start.27 = (f32[4,8,1024]{2,1,0:T(8,128)S(1)}, f32[4,8,1024]{2,1,0:T(8,128)S(1)}, u32[]{:S(2)}, u32[]{:S(2)}) collective-permute-start(f32[4,8,1024]{2,1,0:T(8,128)S(1)} %collective-permute-done.17.refs_2_), channel_id=1, source_target_pairs={{0,16},{16,0},{1,17},{17,1},{2,18},{18,2},{3,19},{19,3},{4,20},{20... | collective-permute-start | bytes 393224 | tf_op jit(solution)/shard_map/ppermute | solution.py:354
  71.7 8.8 %collective-permute-start.26 = (f32[4,8,1024]{2,1,0:T(8,128)S(1)}, f32[4,8,1024]{2,1,0:T(8,128)S(1)}, u32[]{:S(2)}, u32[]{:S(2)}) collective-permute-start(f32[4,8,1024]{2,1,0:T(8,128)S(1)} %collective-permute-done.16.refs_1_), channel_id=1, source_target_pairs={{0,16},{16,0},{1,17},{17,1},{2,18},{18,2},{3,19},{19,3},{4,20},{20... | collective-permute-start | bytes 393224 | tf_op jit(solution)/shard_map/ppermute | solution.py:354
